TPU v7x, 32 devices: a whole 2x2x4 slice. The times are simulated.
32 devices in a mesh: tm: 16 (over z, y, x), head: 2 (over core).
Axes of the slice: x: 2, y: 2, z: 4, core: 2. Of those that a mesh axis runs over, the one named last changes fastest.
Arguments:
- query: bfloat16 [8192, 5120], P('tm', 'head'), may hold values from -100 to 100
- key: bfloat16 [8192, 5120], P('tm', 'head'), may hold values from -100 to 100
- value: bfloat16 [8192, 5120], P('tm', 'head'), may hold values from -6 to 6
- q_gain: float32 [5120], P('head'), may hold values from 0.1 to 1.9
- k_gain: float32 [5120], P('head'), may hold values from 0.1 to 1.9
- far_frames: int32 [128, 12], replicated, may hold values from -1 to 15, as said below
- far_pick: int32 [16, 16], replicated, may hold values from 0 to 7
Outputs:
- attended: bfloat16 [8192, 5120], P('tm', 'head')
Inputs may be any that keep to these rules, and one draw needn't show every extreme that they name: `far_frames`: for query block r of frame f, entry j - 1 (j = 1 to 6) is a frame f - d and entry 5 + j a frame f + d, with 2**j <= d < 2**(j+1), or -1 where no frame of the video lies at such a distance on that side. In the first query block of each frame every such entry is the farthest frame that the band allows on that side.
All inputs are finite; a program needn't handle non-finite values.
Results may differ from a plain program's by a relative error of at most 0.012.
The roundings to bfloat16 on the way count: a program that leaves them out, or rounds other values in their place, can miss the bound.
Values may be sent and summed in bfloat16 or wider, within the bound.
No kernel may reach another device: no remote copies, remote signals or barrier semaphores. Data moves between devices by JAX's collectives and lax.ppermute only.
A program may use at most 128 MiB of HBM per device.

v0:
```python
import functools
import math

import jax
import jax.numpy as jnp
from jax import lax
from jax.experimental import pallas as pl
from jax.experimental.pallas import tpu as pltpu
from jax.sharding import PartitionSpec as P

HEAD_DIM = 128
BLOCK = 64
NFAR = 12
EPSILON = 1e-06
MASKED = -1e30
VMEM_LIMIT = 56 * 1024 * 1024


class Plan:
    def __init__(self, frames, rows, heads):
        self.frames, self.rows = frames, rows
        self.group = 4 if heads % 4 == 0 and frames % 4 == 0 else 1
        self.planes = frames // self.group
        self.blocks = rows // BLOCK
        self.heads = heads // self.group
        bands = sum(2**band <= frames - 1 for band in range(1, NFAR // 2 + 1))
        self.slots = [*range(bands), *range(NFAR // 2, NFAR // 2 + bands)]
        self.square = self.group * self.group
        self.near0 = self.blocks
        self.far0 = self.blocks * (self.group + 2)
        self.total = self.far0 + self.planes * self.square

    def halo(self, step):
        step *= self.group
        return [(i, i + step) for i in range(self.frames) if 0 <= i + step < self.frames]

    def swap(self, j):
        g = self.group
        return [(i, i // g * g + (i % g ^ j)) for i in range(self.frames)]

    def lines(self):
        g = self.group
        return [[p * g + i for p in range(self.planes)] for i in range(g)]


def params():
    return dict(
        compiler_params=pltpu.CompilerParams(vmem_limit_bytes=VMEM_LIMIT),
        cost_estimate=pl.CostEstimate(flops=1, bytes_accessed=1, transcendentals=0),
    )


def select_body(scaled, n_after, group, place_ref, *refs):
    outs = refs[len(refs) - group :]
    refs = list(refs[: len(refs) - group - n_after])
    values = []
    for with_scale in scaled:
        x = refs.pop(0)[...]
        if with_scale:
            rs, gain = refs.pop(0), refs.pop(0)
            x = x.astype(jnp.float32) * rs[...] * gain[...]
        values.append(x.astype(jnp.bfloat16))
    for j, out in enumerate(outs):

        @pl.when(pl.program_id(0) == j)
        def _(out=out):
            for item, x in enumerate(values):
                out[item] = x


def select(plan, place, items, after):
    args, specs = [], []
    for x, head, rs, gain in items:

        def at(j, place, head=head):
            return 0, (place[1] ^ j) * plan.heads + head

        args.append(x)
        specs.append(pl.BlockSpec((plan.rows, HEAD_DIM), at))
        if rs is not None:
            args += [rs, gain]
            specs.append(pl.BlockSpec((plan.rows, 1), lambda j, place: (0, 0)))
            specs.append(pl.BlockSpec((1, HEAD_DIM), at))
    shape = (len(items), plan.rows, HEAD_DIM)
    scaled = [rs is not None for _, _, rs, _ in items]
    return pl.pallas_call(
        functools.partial(select_body, scaled, len(after), plan.group),
        grid_spec=pltpu.PrefetchScalarGridSpec(
            num_scalar_prefetch=1,
            grid=(plan.group,),
            in_specs=specs + [pl.BlockSpec(memory_space=pl.ANY)] * len(after),
            out_specs=[pl.BlockSpec(shape, lambda j, place: (0, 0, 0))] * plan.group,
        ),
        out_shape=[jax.ShapeDtypeStruct(shape, jnp.bfloat16)] * plan.group,
        name="select",
        **params(),
    )(place, *args, *after)


def pack_body(plan, n_after, place_ref, pick_ref, *refs):
    group, blocks = plan.group, plan.blocks
    xs = refs[:group]
    far, to_next, to_prev, sem = refs[group + n_after :]
    plane, lane = place_ref[0], place_ref[1]

    def copies(dest):
        made = []
        for f in range(group):
            for j in range(group):
                g = lane ^ j
                block = pick_ref[(dest * group + f) * plan.frames + plane * group + g]
                src = pl.ds(pl.multiple_of(block * BLOCK, BLOCK), BLOCK)
                dst = pl.ds(pl.multiple_of((f * group + g) * BLOCK, BLOCK), BLOCK)
                made.append(
                    pltpu.make_async_copy(
                        xs[j].at[:, src, :], far.at[dest, :, dst, :], sem.at[dest, len(made)]
                    )
                )
        return made

    def halo(act):
        for j in range(group):
            for at, (g, out) in enumerate(((group - 1, to_next), (0, to_prev))):

                @pl.when((lane ^ j) == g)
                def _(j=j, at=at, out=out):
                    act(pltpu.make_async_copy(xs[j], out, sem.at[plan.planes, at]))

    def for_each(act):
        halo(act)

        def one_plane(dest, carry):
            @pl.when(dest != plane)
            def _():
                for copy in copies(dest):
                    act(copy)

            return carry

        lax.fori_loop(0, plan.planes, one_plane, 0)

    for_each(lambda copy: copy.start())
    for_each(lambda copy: copy.wait())


def pack(plan, place, picks, xs, pair, after):
    smem = pl.BlockSpec(memory_space=pltpu.SMEM)
    any_spec = pl.BlockSpec(memory_space=pl.ANY)
    frame = jax.ShapeDtypeStruct((2, plan.rows, HEAD_DIM), jnp.bfloat16)
    far = jax.ShapeDtypeStruct((plan.planes, 2, plan.square * BLOCK, HEAD_DIM), jnp.bfloat16)
    return pl.pallas_call(
        functools.partial(pack_body, plan, len(after)),
        grid=(1,),
        in_specs=[smem, smem]
        + [pl.BlockSpec((2, plan.rows, HEAD_DIM), lambda i: (pair, 0, 0))] * plan.group
        + [any_spec] * len(after),
        out_specs=[any_spec] * 3,
        out_shape=[far, frame, frame],
        scratch_shapes=[pltpu.SemaphoreType.DMA((plan.planes + 1, max(plan.square, 2)))],
        name="pack",
        **params(),
    )(place, picks, *xs, *after)


def attend_body(plan, heads, at_out, n_out, *refs):
    place_ref, pos_ref = refs[:2]
    group, rows, nfar = plan.group, plan.rows, len(plan.slots)
    step = 2 * group + 3
    inputs = [refs[2 + h * step : 2 + (h + 1) * step] for h in range(len(heads))]
    refs = refs[2 + len(heads) * step + n_out :]
    outs, (qbuf, kvbuf, obuf, fark, farv, sem, out_sem) = refs[:group], refs[group:]
    plane, lane = place_ref[0], place_ref[1]
    scale = math.log2(math.e) / math.sqrt(HEAD_DIM)
    tile = min(rows, 256)
    per_tile = tile // BLOCK
    lanes = lax.broadcasted_iota(jnp.int32, (1, nfar * BLOCK), 1) // BLOCK
    contract = (((1,), (1,)), ((), ()))

    def copies(h):
        made, slot = [], h % 2
        qs, kvs, recvs = inputs[h][:group], inputs[h][group : 2 * group], inputs[h][2 * group :]
        at_q, at_k = heads[h]

        def add(src, dst):
            made.append(pltpu.make_async_copy(src, dst, sem.at[slot, len(made)]))

        def at(first, count):
            first = first * BLOCK
            if not isinstance(first, int):
                first = pl.multiple_of(first, BLOCK)
            return kvbuf.at[slot, :, pl.ds(first, count * BLOCK), :]

        for j in range(group):
            g = lane ^ j
            add(qs[j].at[at_q], qbuf.at[slot, g])
            add(kvs[j].at[at_k : at_k + 2], at(plan.near0 + g * plan.blocks, plan.blocks))
        far, before, after = recvs
        add(before, at(0, plan.blocks))
        add(after, at(plan.near0 + group * plan.blocks, plan.blocks))
        for p in range(plan.planes):
            add(far.at[p], at(plan.far0 + p * plan.square, plan.square))
        return made

    def one_frame(f, h):
        slot = h % 2
        first = pl.multiple_of((plan.near0 + (f - 1) * plan.blocks) * BLOCK, BLOCK)
        frame = plane * group + f
        for t in range(rows // tile):
            q = qbuf[slot, f, t * tile : (t + 1) * tile, :]
            scores = []
            for part, ok in enumerate((frame > 0, None, frame < plan.frames - 1)):
                k = kvbuf[slot, 0, pl.ds(first + part * rows, rows), :]
                s = lax.dot_general(q, k, contract, preferred_element_type=jnp.float32)
                scores.append(s if ok is None else jnp.where(ok, s, MASKED))
            far = []
            for i in range(per_tile):
                block = t * per_tile + i
                ok = lanes < 0
                for n in range(nfar):
                    at = pos_ref[(f * plan.blocks + block) * nfar + n]
                    src = pl.ds(pl.multiple_of(jnp.maximum(at, 0) * BLOCK, BLOCK), BLOCK)
                    fark[block, n * BLOCK : (n + 1) * BLOCK, :] = kvbuf[slot, 0, src, :]
                    farv[block, n * BLOCK : (n + 1) * BLOCK, :] = kvbuf[slot, 1, src, :]
                    ok = ok | ((lanes == n) & (at >= 0))
                s = lax.dot_general(
                    q[i * BLOCK : (i + 1) * BLOCK],
                    fark[block],
                    contract,
                    preferred_element_type=jnp.float32,
                )
                far.append(jnp.where(ok, s, MASKED))
            far = jnp.concatenate(far, axis=0)
            peak = jnp.max(far, axis=1, keepdims=True)
            for s in scores:
                peak = jnp.maximum(peak, jnp.max(s, axis=1, keepdims=True))
            total, out = 0.0, 0.0
            for part, s in enumerate(scores):
                p = jnp.exp2((s - peak) * scale)
                total += jnp.sum(p, axis=1, keepdims=True)
                v = kvbuf[slot, 1, pl.ds(first + part * rows, rows), :]
                out += jnp.dot(p.astype(jnp.bfloat16), v, preferred_element_type=jnp.float32)
            p = jnp.exp2((far - peak) * scale)
            total += jnp.sum(p, axis=1, keepdims=True)
            p = p.astype(jnp.bfloat16)
            far_out = [
                jnp.dot(
                    p[i * BLOCK : (i + 1) * BLOCK],
                    farv[t * per_tile + i],
                    preferred_element_type=jnp.float32,
                )
                for i in range(per_tile)
            ]
            out = (out + jnp.concatenate(far_out, axis=0)) / total
            obuf[f, h, t * tile : (t + 1) * tile, :] = out.astype(jnp.bfloat16)

    for copy in copies(0):
        copy.start()
    for h in range(len(heads)):
        if h + 1 < len(heads):
            for copy in copies(h + 1):
                copy.start()
        for copy in copies(h):
            copy.wait()
        lax.fori_loop(0, group, lambda f, c, h=h: (one_frame(f, h), c)[1], 0)
    made = []
    for j in range(group):
        dst = outs[j].at[at_out : at_out + len(heads)]
        made.append(pltpu.make_async_copy(obuf.at[lane ^ j], dst, out_sem.at[j]))
    for copy in made:
        copy.start()
    for copy in made:
        copy.wait()


def attend(plan, place, pos, heads, at_out, of, outs):
    nfar, count = len(plan.slots), len(heads)
    any_spec = pl.BlockSpec(memory_space=pl.ANY)
    smem = pl.BlockSpec(memory_space=pltpu.SMEM)
    args = [y for q, _, kv, _, recv in heads for y in (*q, *kv, *recv)]
    items = [(at_q, at_k) for _, at_q, _, at_k, _ in heads]
    shape = jax.ShapeDtypeStruct((of, plan.rows, HEAD_DIM), jnp.bfloat16)
    return pl.pallas_call(
        functools.partial(attend_body, plan, items, at_out, len(outs)),
        in_specs=[smem, smem] + [any_spec] * (len(args) + len(outs)),
        out_specs=[any_spec] * plan.group,
        out_shape=[shape] * plan.group,
        input_output_aliases={2 + len(args) + j: j for j in range(len(outs))},
        scratch_shapes=[
            pltpu.VMEM((2, plan.group, plan.rows, HEAD_DIM), jnp.bfloat16),
            pltpu.VMEM((2, 2, plan.total * BLOCK, HEAD_DIM), jnp.bfloat16),
            pltpu.VMEM((plan.group, count, plan.rows, HEAD_DIM), jnp.bfloat16),
            pltpu.VMEM((plan.blocks, nfar * BLOCK, HEAD_DIM), jnp.bfloat16),
            pltpu.VMEM((plan.blocks, nfar * BLOCK, HEAD_DIM), jnp.bfloat16),
            pltpu.SemaphoreType.DMA((2, 2 * plan.group + 2 + plan.planes)),
            pltpu.SemaphoreType.DMA((plan.group,)),
        ],
        name="attend",
        **params(),
    )(place, pos, *args, *outs)


def merge_body(plan, first, place_ref, *refs):
    xs, (out, sem) = refs[: plan.group], refs[-2:]
    copies = []
    for j, x in enumerate(xs):
        for h in range(x.shape[0]):
            start = ((place_ref[1] ^ j) * plan.heads + first + h) * HEAD_DIM
            dst = out.at[:, pl.ds(pl.multiple_of(start, HEAD_DIM), HEAD_DIM)]
            copies.append(pltpu.make_async_copy(x.at[h], dst, sem.at[len(copies)]))
    for copy in copies:
        copy.start()
    for copy in copies:
        copy.wait()


def merge(plan, place, xs, first, out):
    width = plan.group * plan.heads * HEAD_DIM
    any_spec = pl.BlockSpec(memory_space=pl.ANY)
    vmem = pl.BlockSpec(memory_space=pltpu.VMEM)
    return pl.pallas_call(
        functools.partial(merge_body, plan, first),
        in_specs=[pl.BlockSpec(memory_space=pltpu.SMEM)]
        + [vmem] * plan.group
        + [any_spec] * len(out),
        out_specs=any_spec,
        out_shape=jax.ShapeDtypeStruct((plan.rows, width), jnp.bfloat16),
        input_output_aliases={1 + plan.group: 0} if out else {},
        scratch_shapes=[pltpu.SemaphoreType.DMA((plan.group * xs[0].shape[0],))],
        name="merge",
        **params(),
    )(place, *xs, *out)


def far_positions(plan, plane, far_frames, far_pick):
    group, blocks = plan.group, plan.blocks
    own = group * blocks
    lists = lax.dynamic_slice_in_dim(far_frames, plane * own, own, 0)
    lists = jnp.concatenate([lists[:, s : s + 1] for s in plan.slots], axis=1)
    g = jnp.maximum(lists, 0)
    rows = lax.dynamic_slice_in_dim(far_pick, plane * group, group, 0)
    rows = jnp.repeat(rows, blocks, axis=0)
    hit = g[:, :, None] == jnp.arange(plan.frames)
    pick = jnp.sum(jnp.where(hit, rows[:, None, :], 0), axis=2)
    f = (jnp.arange(own) // blocks)[:, None]
    source, lane = g // group, g % group
    pos = plan.far0 + (source * group + f) * group + lane
    away = g - plane * group
    near = (away >= -1) & (away <= group)
    pos = jnp.where(near, plan.near0 + away * blocks + pick, pos)
    return jnp.where(lists >= 0, pos, -1).astype(jnp.int32).reshape(-1)


def local(query, key, value, q_gain, k_gain, far_frames, far_pick):
    rows, width = query.shape
    full_width = width * lax.axis_size("head")
    plan = Plan(lax.axis_size("tm"), rows, width // HEAD_DIM)
    frame = lax.axis_index("tm").astype(jnp.int32)
    plane = frame // plan.group
    place = jnp.stack([plane, frame % plan.group])
    picks = far_pick.reshape(-1)

    def share(xs):
        return [xs[0]] + [lax.ppermute(xs[j], "tm", plan.swap(j)) for j in range(1, plan.group)]

    def exchange(xs, pair, after):
        far, to_next, to_prev = pack(plan, place, picks, xs, pair, after)
        packed.append([far])
        return (
            lax.all_to_all(far, "tm", 0, 0, axis_index_groups=plan.lines(), tiled=True),
            lax.ppermute(to_next, "tm", plan.halo(1)),
            lax.ppermute(to_prev, "tm", plan.halo(-1)),
        )

    sums = jnp.stack([jnp.sum(jnp.square(x.astype(jnp.float32)), axis=1) for x in (query, key)])
    q_rs, k_rs = lax.rsqrt(lax.psum(sums, "head") / full_width + EPSILON)[:, :, None]
    q_gain, k_gain = q_gain[None, :], k_gain[None, :]

    def pair(h):
        return [(key, h, k_rs, k_gain), (value, h, None, None)]

    heads = plan.heads
    queries = [(query, h, q_rs, q_gain) for h in range(heads)]
    rounds = [[h] for h in range(min(2, heads))]
    if heads > 3:
        rounds.append(list(range(2, heads - 1)))
    if heads > 2:
        rounds.append([heads - 1])
    packed, recvs, where, after = [], [], [], []
    out = None
    for index, chosen in enumerate(rounds):
        items = [item for h in chosen for item in pair(h)]
        ending = index + 1 == len(rounds)
        x = share(select(plan, place, items + (queries if ending else []), after))
        where += [(x, 2 * n) for n in range(len(chosen))]
        if ending:
            q, first_q = x, len(items)
        else:
            for n in range(len(chosen)):
                recvs.append(exchange(x, n, []))
                if n == 0:
                    after = packed[-1]
    pos = far_positions(plan, plane, far_frames, far_pick)

    def run(chosen, at_out, of, out):
        args = [(q, first_q + h, *where[h], recvs[h]) for h in chosen]
        return attend(plan, place, pos, args, at_out, of, out)

    early = min(2, heads - 1)
    if early:
        out = merge(plan, place, share(run(range(early), 0, early, [])), 0, [])
    recvs.append(exchange(x, 0, [out] if early else []))
    held = []
    for h in range(early, heads):
        held = run([h], h - early, heads - early, held)
    return merge(plan, place, share(held), early, [out] if early else [])


def solution(mesh):
    placed = (P("tm", "head"), P("tm", "head"), P("tm", "head"), P("head"), P("head"), P(), P())
    return jax.shard_map(
        local, mesh=mesh, in_specs=placed, out_specs=P("tm", "head"), check_vma=False
    )
```

profile of v0, /device:TPU:16, one launch (start us, length us, event | category | flops | bytes accessed | tf_op | source)
XLA Modules:
  0.0 416.8 jit_solution(6780155044587959978)
XLA Ops:
  7.7 4.5 %select.28 = (bf16[2,512,128]{2,1,0:T(8,128)(2,1)}, bf16[2,512,128]{2,1,0:T(8,128)(2,1)}, bf16[2,512,128]{2,1,0:T(8,128)(2,1)}, bf16[2,512,128]{2,1,0:T(8,128)(2,1)}) custom-call(s32[2]{0:T(128)} %pad_add_fusion.1.place_ref.refs_0_, bf16[512,2560]{1,0:T(8,128)(2,1)} %refs_0_.7, f32[512,1]{1,0:T(8,128)} %copy.63.refs_1_.refs_5_, ...), custom_call_target="tpu_custom_call" | custom-call | flops 1 | bytes 1 | tf_op jit(solution)/shard_map/select/pallas_call | solution.py:86
  16.4 5.2 %collective-permute-done.refs_1_.refs_7_ = bf16[2,512,128]{2,1,0:T(8,128)(2,1)S(1)} collective-permute-done((bf16[2,512,128]{2,1,0:T(8,128)(2,1)}, bf16[2,512,128]{2,1,0:T(8,128)(2,1)S(1)}, u32[]{:S(2)}, u32[]{:S(2)}) %collective-permute-start) | collective-permute-done | bytes 262176 | tf_op jit(solution)/shard_map/ppermute | solution.py:363
  21.6 6.1 %collective-permute-done.1.refs_2_.refs_8_ = bf16[2,512,128]{2,1,0:T(8,128)(2,1)S(1)} collective-permute-done((bf16[2,512,128]{2,1,0:T(8,128)(2,1)}, bf16[2,512,128]{2,1,0:T(8,128)(2,1)S(1)}, u32[]{:S(2)}, u32[]{:S(2)}) %collective-permute-start.1) | collective-permute-done | bytes 262176 | tf_op jit(solution)/shard_map/ppermute | solution.py:363
  31.7 5.2 %all-to-all-start = ((bf16[4,2,1024,128]{3,2,1,0:T(8,128)(2,1)}), bf16[4,2,1024,128]{3,2,1,0:T(8,128)(2,1)S(1)}, u32[]{:S(2)}, u32[]{:S(2)}) async-start(bf16[4,2,1024,128]{3,2,1,0:T(8,128)(2,1)} %get-tuple-element.56.refs_4_), calls=%async_computation | async-start | bytes 4194304 | tf_op jit(solution)/shard_map/all_to_all | solution.py:369
  44.8 6.0 %collective-permute-done.3.refs_1_.refs_18_ = bf16[2,512,128]{2,1,0:T(8,128)(2,1)S(1)} collective-permute-done((bf16[2,512,128]{2,1,0:T(8,128)(2,1)}, bf16[2,512,128]{2,1,0:T(8,128)(2,1)S(1)}, u32[]{:S(2)}, u32[]{:S(2)}) %collective-permute-start.3) | collective-permute-done | bytes 262176 | tf_op jit(solution)/shard_map/ppermute | solution.py:363
  59.0 21.9 %all-to-all-done.refs_10_ = bf16[4,2,1024,128]{3,2,1,0:T(8,128)(2,1)S(1)} async-done(((bf16[4,2,1024,128]{3,2,1,0:T(8,128)(2,1)}), bf16[4,2,1024,128]{3,2,1,0:T(8,128)(2,1)S(1)}, u32[]{:S(2)}, u32[]{:S(2)}) %all-to-all-start) | async-done | bytes 2097184 | tf_op jit(solution)/shard_map/all_to_all | solution.py:369
  81.0 7.7 %all-to-all-start.1 = ((bf16[4,2,1024,128]{3,2,1,0:T(8,128)(2,1)}), bf16[4,2,1024,128]{3,2,1,0:T(8,128)(2,1)}, u32[]{:S(2)}, u32[]{:S(2)}) async-start(bf16[4,2,1024,128]{3,2,1,0:T(8,128)(2,1)} %get-tuple-element.61.refs_8_), calls=%async_computation.1 | async-start | bytes 4194304 | tf_op jit(solution)/shard_map/all_to_all | solution.py:369
  88.7 5.6 %select.30 = (bf16[4,512,128]{2,1,0:T(8,128)(2,1)}, bf16[4,512,128]{2,1,0:T(8,128)(2,1)}, bf16[4,512,128]{2,1,0:T(8,128)(2,1)}, bf16[4,512,128]{2,1,0:T(8,128)(2,1)}) custom-call(s32[2]{0:T(128)} %pad_add_fusion.1.place_ref.refs_0_, bf16[512,2560]{1,0:T(8,128)(2,1)} %refs_0_.7, f32[512,1]{1,0:T(8,128)} %copy.63.refs_1_.refs_5_, ...), custom_call_target="tpu_custom_call" | custom-call | flops 1 | bytes 1 | tf_op jit(solution)/shard_map/select/pallas_call | solution.py:86
  97.8 11.6 %collective-permute-done.6.refs_1_.refs_7_ = bf16[4,512,128]{2,1,0:T(8,128)(2,1)S(1)} collective-permute-done((bf16[4,512,128]{2,1,0:T(8,128)(2,1)}, bf16[4,512,128]{2,1,0:T(8,128)(2,1)S(1)}, u32[]{:S(2)}, u32[]{:S(2)}) %collective-permute-start.6) | collective-permute-done | bytes 524320 | tf_op jit(solution)/shard_map/ppermute | solution.py:363
  109.4 10.2 %collective-permute-done.7.refs_2_.refs_8_ = bf16[4,512,128]{2,1,0:T(8,128)(2,1)S(1)} collective-permute-done((bf16[4,512,128]{2,1,0:T(8,128)(2,1)}, bf16[4,512,128]{2,1,0:T(8,128)(2,1)S(1)}, u32[]{:S(2)}, u32[]{:S(2)}) %collective-permute-start.7) | collective-permute-done | bytes 524320 | tf_op jit(solution)/shard_map/ppermute | solution.py:363
  123.8 9.2 %all-to-all-done.1.refs_21_ = bf16[4,2,1024,128]{3,2,1,0:T(8,128)(2,1)} async-done(((bf16[4,2,1024,128]{3,2,1,0:T(8,128)(2,1)}), bf16[4,2,1024,128]{3,2,1,0:T(8,128)(2,1)}, u32[]{:S(2)}, u32[]{:S(2)}) %all-to-all-start.1) | async-done | bytes 2097184 | tf_op jit(solution)/shard_map/all_to_all | solution.py:369
  133.1 7.0 %all-to-all-start.3 = ((bf16[4,2,1024,128]{3,2,1,0:T(8,128)(2,1)}), bf16[4,2,1024,128]{3,2,1,0:T(8,128)(2,1)S(1)}, u32[]{:S(2)}, u32[]{:S(2)}) async-start(bf16[4,2,1024,128]{3,2,1,0:T(8,128)(2,1)} %get-tuple-element.82), calls=%async_computation.3 | async-start | bytes 4194304 | tf_op jit(solution)/shard_map/all_to_all | solution.py:369
  143.4 41.1 %all-to-all-done.3.refs_10_ = bf16[4,2,1024,128]{3,2,1,0:T(8,128)(2,1)S(1)} async-done(((bf16[4,2,1024,128]{3,2,1,0:T(8,128)(2,1)}), bf16[4,2,1024,128]{3,2,1,0:T(8,128)(2,1)S(1)}, u32[]{:S(2)}, u32[]{:S(2)}) %all-to-all-start.3) | async-done | bytes 2097184 | tf_op jit(solution)/shard_map/all_to_all | solution.py:369
  184.5 7.7 %all-to-all-start.4 = ((bf16[4,2,1024,128]{3,2,1,0:T(8,128)(2,1)}), bf16[4,2,1024,128]{3,2,1,0:T(8,128)(2,1)}, u32[]{:S(2)}, u32[]{:S(2)}) async-start(bf16[4,2,1024,128]{3,2,1,0:T(8,128)(2,1)} %get-tuple-element.66.refs_19_), calls=%async_computation.4 | async-start | bytes 4194304 | tf_op jit(solution)/shard_map/all_to_all | solution.py:369
  193.6 8.2 %select.31 = (bf16[7,512,128]{2,1,0:T(8,128)(2,1)}, bf16[7,512,128]{2,1,0:T(8,128)(2,1)}, bf16[7,512,128]{2,1,0:T(8,128)(2,1)}, bf16[7,512,128]{2,1,0:T(8,128)(2,1)}) custom-call(s32[2]{0:T(128)} %pad_add_fusion.1.place_ref.refs_0_, bf16[512,2560]{1,0:T(8,128)(2,1)} %refs_0_.7, f32[512,1]{1,0:T(8,128)} %copy.63.refs_1_.refs_5_, ...), custom_call_target="tpu_custom_call" | custom-call | flops 1 | bytes 1 | tf_op jit(solution)/shard_map/select/pallas_call | solution.py:86
  212.6 30.5 %collective-permute-done.12.refs_11_ = bf16[2,512,128]{2,1,0:T(8,128)(2,1)S(1)} collective-permute-done((bf16[2,512,128]{2,1,0:T(8,128)(2,1)}, bf16[2,512,128]{2,1,0:T(8,128)(2,1)S(1)}, u32[]{:S(2)}, u32[]{:S(2)}) %collective-permute-start.12) | collective-permute-done | bytes 262176 | tf_op jit(solution)/shard_map/ppermute | solution.py:370
  260.8 20.7 %attend.4 = (bf16[2,512,128]{2,1,0:T(8,128)(2,1)}, bf16[2,512,128]{2,1,0:T(8,128)(2,1)}, bf16[2,512,128]{2,1,0:T(8,128)(2,1)}, bf16[2,512,128]{2,1,0:T(8,128)(2,1)}) custom-call(s32[2]{0:T(128)} %pad_add_fusion.1.place_ref.refs_0_, s32[192]{0:T(256)} %fusion.6.refs_1_, bf16[7,512,128]{2,1,0:T(8,128)(2,1)} %get-tuple-element.67.refs_2_.refs_13_.refs_0_.refs_6_, ...), custom_call_target="tpu_custom_call" | custom-call | flops 1 | bytes 1 | tf_op jit(solution)/shard_map/attend/pallas_call | solution.py:282
  285.0 5.3 %collective-permute-done.16.refs_1_ = bf16[2,512,128]{2,1,0:T(8,128)(2,1)S(1)} collective-permute-done((bf16[2,512,128]{2,1,0:T(8,128)(2,1)}, bf16[2,512,128]{2,1,0:T(8,128)(2,1)S(1)}, u32[]{:S(2)}, u32[]{:S(2)}) %collective-permute-start.16) | collective-permute-done | bytes 262176 | tf_op jit(solution)/shard_map/ppermute | solution.py:363
  300.7 4.6 %all-to-all-start.2 = ((bf16[4,2,1024,128]{3,2,1,0:T(8,128)(2,1)}), bf16[4,2,1024,128]{3,2,1,0:T(8,128)(2,1)S(1)}, u32[]{:S(2)}, u32[]{:S(2)}) async-start(bf16[4,2,1024,128]{3,2,1,0:T(8,128)(2,1)} %get-tuple-element.79), calls=%async_computation.2 | async-start | bytes 4194304 | tf_op jit(solution)/shard_map/all_to_all | solution.py:369
  320.5 37.8 %collective-permute-done.23.refs_11_ = bf16[2,512,128]{2,1,0:T(8,128)(2,1)S(1)} collective-permute-done((bf16[2,512,128]{2,1,0:T(8,128)(2,1)S(1)}, bf16[2,512,128]{2,1,0:T(8,128)(2,1)S(1)}, u32[]{:S(2)}, u32[]{:S(2)}) %collective-permute-start.23) | collective-permute-done | bytes 262176 | tf_op jit(solution)/shard_map/ppermute | solution.py:370
  361.2 12.3 %attend.5 = (bf16[3,512,128]{2,1,0:T(8,128)(2,1)}, bf16[3,512,128]{2,1,0:T(8,128)(2,1)}, bf16[3,512,128]{2,1,0:T(8,128)(2,1)}, bf16[3,512,128]{2,1,0:T(8,128)(2,1)}) custom-call(s32[2]{0:T(128)} %pad_add_fusion.1.place_ref.refs_0_, s32[192]{0:T(256)} %fusion.6.refs_1_, bf16[7,512,128]{2,1,0:T(8,128)(2,1)} %get-tuple-element.67.refs_2_.refs_13_.refs_0_.refs_6_, ...), custom_call_target="tpu_custom_call" | custom-call | flops 1 | bytes 1 | tf_op jit(solution)/shard_map/attend/pallas_call | solution.py:282
  374.3 12.3 %attend.6 = (bf16[3,512,128]{2,1,0:T(8,128)(2,1)}, bf16[3,512,128]{2,1,0:T(8,128)(2,1)}, bf16[3,512,128]{2,1,0:T(8,128)(2,1)}, bf16[3,512,128]{2,1,0:T(8,128)(2,1)}) custom-call(s32[2]{0:T(128)} %pad_add_fusion.1.place_ref.refs_0_, s32[192]{0:T(256)} %fusion.6.refs_1_, ...), custom_call_target="tpu_custom_call", output_to_operand_aliasing={{0}: (13, {}), {1}: (14, {}), {2}: (15, {}), {3}: (16, {})} | custom-call | flops 1 | bytes 1 | tf_op jit(solution)/shard_map/attend/pallas_call | solution.py:282
  388.1 12.3 %attend.7 = (bf16[3,512,128]{2,1,0:T(8,128)(2,1)}, bf16[3,512,128]{2,1,0:T(8,128)(2,1)}, bf16[3,512,128]{2,1,0:T(8,128)(2,1)}, bf16[3,512,128]{2,1,0:T(8,128)(2,1)}) custom-call(s32[2]{0:T(128)} %pad_add_fusion.1.place_ref.refs_0_, s32[192]{0:T(256)} %fusion.6.refs_1_, ...), custom_call_target="tpu_custom_call", output_to_operand_aliasing={{0}: (13, {}), {1}: (14, {}), {2}: (15, {}), {3}: (16, {})} | custom-call | flops 1 | bytes 1 | tf_op jit(solution)/shard_map/attend/pallas_call | solution.py:282
  408.4 4.8 %collective-permute-done.26.refs_2_ = bf16[3,512,128]{2,1,0:T(8,128)(2,1)S(1)} collective-permute-done((bf16[3,512,128]{2,1,0:T(8,128)(2,1)}, bf16[3,512,128]{2,1,0:T(8,128)(2,1)S(1)}, u32[]{:S(2)}, u32[]{:S(2)}) %collective-permute-start.26) | collective-permute-done | bytes 393248 | tf_op jit(solution)/shard_map/ppermute | solution.py:363
  (171 shorter events, 118.5 us)
Async XLA Ops:
  13.7 13.9 %collective-permute-start.1 = (bf16[2,512,128]{2,1,0:T(8,128)(2,1)}, bf16[2,512,128]{2,1,0:T(8,128)(2,1)S(1)}, u32[]{:S(2)}, u32[]{:S(2)}) collective-permute-start(bf16[2,512,128]{2,1,0:T(8,128)(2,1)} %get-tuple-element.54), channel_id=1, source_target_pairs={{0,4},{2,6},{4,0},{6,2},{8,12},{10,14},{12,8},{14,10},{16,20},{18,... | collective-permute-start | bytes 786440 | tf_op jit(solution)/shard_map/ppermute | solution.py:363
  15.2 12.4 %collective-permute-start.2 = (bf16[2,512,128]{2,1,0:T(8,128)(2,1)}, bf16[2,512,128]{2,1,0:T(8,128)(2,1)S(1)}, u32[]{:S(2)}, u32[]{:S(2)}) collective-permute-start(bf16[2,512,128]{2,1,0:T(8,128)(2,1)} %get-tuple-element.55), channel_id=1, source_target_pairs={{0,6},{2,4},{4,2},{6,0},{8,14},{10,12},{12,10},{14,8},{16,22},{18,... | collective-permute-start | bytes 786440 | tf_op jit(solution)/shard_map/ppermute | solution.py:363
  31.7 49.3 %all-to-all-start = ((bf16[4,2,1024,128]{3,2,1,0:T(8,128)(2,1)}), bf16[4,2,1024,128]{3,2,1,0:T(8,128)(2,1)S(1)}, u32[]{:S(2)}, u32[]{:S(2)}) async-start(bf16[4,2,1024,128]{3,2,1,0:T(8,128)(2,1)} %get-tuple-element.56.refs_4_), calls=%async_computation | async-start | bytes 4194304 | tf_op jit(solution)/shard_map/all_to_all | solution.py:369
  42.4 12.5 %collective-permute-start.4 = (bf16[2,512,128]{2,1,0:T(8,128)(2,1)}, bf16[2,512,128]{2,1,0:T(8,128)(2,1)S(1)}, u32[]{:S(2)}, u32[]{:S(2)}) collective-permute-start(bf16[2,512,128]{2,1,0:T(8,128)(2,1)} %get-tuple-element.59), channel_id=1, source_target_pairs={{0,4},{2,6},{4,0},{6,2},{8,12},{10,14},{12,8},{14,10},{16,20},{18,... | collective-permute-start | bytes 786440 | tf_op jit(solution)/shard_map/ppermute | solution.py:363
  81.0 52.1 %all-to-all-start.1 = ((bf16[4,2,1024,128]{3,2,1,0:T(8,128)(2,1)}), bf16[4,2,1024,128]{3,2,1,0:T(8,128)(2,1)}, u32[]{:S(2)}, u32[]{:S(2)}) async-start(bf16[4,2,1024,128]{3,2,1,0:T(8,128)(2,1)} %get-tuple-element.61.refs_8_), calls=%async_computation.1 | async-start | bytes 4194304 | tf_op jit(solution)/shard_map/all_to_all | solution.py:369
  94.2 15.1 %collective-permute-start.6 = (bf16[4,512,128]{2,1,0:T(8,128)(2,1)}, bf16[4,512,128]{2,1,0:T(8,128)(2,1)S(1)}, u32[]{:S(2)}, u32[]{:S(2)}) collective-permute-start(bf16[4,512,128]{2,1,0:T(8,128)(2,1)} %get-tuple-element.63), channel_id=1, source_target_pairs={{0,2},{2,0},{4,6},{6,4},{8,10},{10,8},{12,14},{14,12},{16,18},{18,... | collective-permute-start | bytes 1572872 | tf_op jit(solution)/shard_map/ppermute | solution.py:363
  95.8 23.8 %collective-permute-start.7 = (bf16[4,512,128]{2,1,0:T(8,128)(2,1)}, bf16[4,512,128]{2,1,0:T(8,128)(2,1)S(1)}, u32[]{:S(2)}, u32[]{:S(2)}) collective-permute-start(bf16[4,512,128]{2,1,0:T(8,128)(2,1)} %get-tuple-element.64), channel_id=1, source_target_pairs={{0,4},{2,6},{4,0},{6,2},{8,12},{10,14},{12,8},{14,10},{16,20},{18,... | collective-permute-start | bytes 1572872 | tf_op jit(solution)/shard_map/ppermute | solution.py:363
  96.3 23.3 %collective-permute-start.8 = (bf16[4,512,128]{2,1,0:T(8,128)(2,1)}, bf16[4,512,128]{2,1,0:T(8,128)(2,1)S(1)}, u32[]{:S(2)}, u32[]{:S(2)}) collective-permute-start(bf16[4,512,128]{2,1,0:T(8,128)(2,1)} %get-tuple-element.65), channel_id=1, source_target_pairs={{0,6},{2,4},{4,2},{6,0},{8,14},{10,12},{12,10},{14,8},{16,22},{18,... | collective-permute-start | bytes 1572872 | tf_op jit(solution)/shard_map/ppermute | solution.py:363
  133.1 51.4 %all-to-all-start.3 = ((bf16[4,2,1024,128]{3,2,1,0:T(8,128)(2,1)}), bf16[4,2,1024,128]{3,2,1,0:T(8,128)(2,1)S(1)}, u32[]{:S(2)}, u32[]{:S(2)}) async-start(bf16[4,2,1024,128]{3,2,1,0:T(8,128)(2,1)} %get-tuple-element.82), calls=%async_computation.3 | async-start | bytes 4194304 | tf_op jit(solution)/shard_map/all_to_all | solution.py:369
  184.5 116.2 %all-to-all-start.4 = ((bf16[4,2,1024,128]{3,2,1,0:T(8,128)(2,1)}), bf16[4,2,1024,128]{3,2,1,0:T(8,128)(2,1)}, u32[]{:S(2)}, u32[]{:S(2)}) async-start(bf16[4,2,1024,128]{3,2,1,0:T(8,128)(2,1)} %get-tuple-element.66.refs_19_), calls=%async_computation.4 | async-start | bytes 4194304 | tf_op jit(solution)/shard_map/all_to_all | solution.py:369
  201.8 57.3 %collective-permute-start.9 = (bf16[7,512,128]{2,1,0:T(8,128)(2,1)}, bf16[7,512,128]{2,1,0:T(8,128)(2,1)S(1)}, u32[]{:S(2)}, u32[]{:S(2)}) collective-permute-start(bf16[7,512,128]{2,1,0:T(8,128)(2,1)} %get-tuple-element.68), channel_id=1, source_target_pairs={{0,2},{2,0},{4,6},{6,4},{8,10},{10,8},{12,14},{14,12},{16,18},{18,... | collective-permute-start | bytes 2752520 | tf_op jit(solution)/shard_map/ppermute | solution.py:363
  203.3 55.8 %collective-permute-start.10 = (bf16[7,512,128]{2,1,0:T(8,128)(2,1)}, bf16[7,512,128]{2,1,0:T(8,128)(2,1)S(1)}, u32[]{:S(2)}, u32[]{:S(2)}) collective-permute-start(bf16[7,512,128]{2,1,0:T(8,128)(2,1)} %get-tuple-element.69), channel_id=1, source_target_pairs={{0,4},{2,6},{4,0},{6,2},{8,12},{10,14},{12,8},{14,10},{16,20},{18,... | collective-permute-start | bytes 2752520 | tf_op jit(solution)/shard_map/ppermute | solution.py:363
  203.9 55.3 %collective-permute-start.11 = (bf16[7,512,128]{2,1,0:T(8,128)(2,1)}, bf16[7,512,128]{2,1,0:T(8,128)(2,1)S(1)}, u32[]{:S(2)}, u32[]{:S(2)}) collective-permute-start(bf16[7,512,128]{2,1,0:T(8,128)(2,1)} %get-tuple-element.70), channel_id=1, source_target_pairs={{0,6},{2,4},{4,2},{6,0},{8,14},{10,12},{12,10},{14,8},{16,22},{18,... | collective-permute-start | bytes 2752520 | tf_op jit(solution)/shard_map/ppermute | solution.py:363
  205.5 37.6 %collective-permute-start.12 = (bf16[2,512,128]{2,1,0:T(8,128)(2,1)}, bf16[2,512,128]{2,1,0:T(8,128)(2,1)S(1)}, u32[]{:S(2)}, u32[]{:S(2)}) collective-permute-start(bf16[2,512,128]{2,1,0:T(8,128)(2,1)} %get-tuple-element.71), channel_id=1, source_target_pairs={{0,8},{2,10},{4,12},{6,14},{8,16},{10,18},{12,20},{14,22},{16,24},... | collective-permute-start | bytes 786440 | tf_op jit(solution)/shard_map/ppermute | solution.py:370
  208.9 36.1 %collective-permute-start.13 = (bf16[2,512,128]{2,1,0:T(8,128)(2,1)}, bf16[2,512,128]{2,1,0:T(8,128)(2,1)S(1)}, u32[]{:S(2)}, u32[]{:S(2)}) collective-permute-start(bf16[2,512,128]{2,1,0:T(8,128)(2,1)} %get-tuple-element.72), channel_id=1, source_target_pairs={{8,0},{10,2},{12,4},{14,6},{16,8},{18,10},{20,12},{22,14},{24,16},... | collective-permute-start | bytes 786440 | tf_op jit(solution)/shard_map/ppermute | solution.py:371
  243.1 16.0 %collective-permute-start.14 = (bf16[2,512,128]{2,1,0:T(8,128)(2,1)}, bf16[2,512,128]{2,1,0:T(8,128)(2,1)S(1)}, u32[]{:S(2)}, u32[]{:S(2)}) collective-permute-start(bf16[2,512,128]{2,1,0:T(8,128)(2,1)} %get-tuple-element.73), channel_id=1, source_target_pairs={{0,8},{2,10},{4,12},{6,14},{8,16},{10,18},{12,20},{14,22},{16,24},... | collective-permute-start | bytes 786440 | tf_op jit(solution)/shard_map/ppermute | solution.py:370
  245.0 14.1 %collective-permute-start.15 = (bf16[2,512,128]{2,1,0:T(8,128)(2,1)}, bf16[2,512,128]{2,1,0:T(8,128)(2,1)}, u32[]{:S(2)}, u32[]{:S(2)}) collective-permute-start(bf16[2,512,128]{2,1,0:T(8,128)(2,1)} %get-tuple-element.74), channel_id=1, source_target_pairs={{8,0},{10,2},{12,4},{14,6},{16,8},{18,10},{20,12},{22,14},{24,16},... | collective-permute-start | bytes 786440 | tf_op jit(solution)/shard_map/ppermute | solution.py:371
  300.7 85.9 %all-to-all-start.2 = ((bf16[4,2,1024,128]{3,2,1,0:T(8,128)(2,1)}), bf16[4,2,1024,128]{3,2,1,0:T(8,128)(2,1)S(1)}, u32[]{:S(2)}, u32[]{:S(2)}) async-start(bf16[4,2,1024,128]{3,2,1,0:T(8,128)(2,1)} %get-tuple-element.79), calls=%async_computation.2 | async-start | bytes 4194304 | tf_op jit(solution)/shard_map/all_to_all | solution.py:369
  305.3 53.0 %collective-permute-start.23 = (bf16[2,512,128]{2,1,0:T(8,128)(2,1)S(1)}, bf16[2,512,128]{2,1,0:T(8,128)(2,1)S(1)}, u32[]{:S(2)}, u32[]{:S(2)}) collective-permute-start(bf16[2,512,128]{2,1,0:T(8,128)(2,1)S(1)} %copy-done.38), channel_id=1, source_target_pairs={{0,8},{2,10},{4,12},{6,14},{8,16},{10,18},{12,20},{14,22},{16,24},... | collective-permute-start | bytes 786440 | tf_op jit(solution)/shard_map/ppermute | solution.py:370
  308.7 51.7 %collective-permute-start.24 = (bf16[2,512,128]{2,1,0:T(8,128)(2,1)S(1)}, bf16[2,512,128]{2,1,0:T(8,128)(2,1)S(1)}, u32[]{:S(2)}, u32[]{:S(2)}) collective-permute-start(bf16[2,512,128]{2,1,0:T(8,128)(2,1)S(1)} %copy-done.37), channel_id=1, source_target_pairs={{8,0},{10,2},{12,4},{14,6},{16,8},{18,10},{20,12},{22,14},{24,16},... | collective-permute-start | bytes 786440 | tf_op jit(solution)/shard_map/ppermute | solution.py:371
  311.2 62.2 %collective-permute-start.21 = (bf16[2,512,128]{2,1,0:T(8,128)(2,1)S(1)}, bf16[2,512,128]{2,1,0:T(8,128)(2,1)S(1)}, u32[]{:S(2)}, u32[]{:S(2)}) collective-permute-start(bf16[2,512,128]{2,1,0:T(8,128)(2,1)S(1)} %copy-done.36), channel_id=1, source_target_pairs={{0,8},{2,10},{4,12},{6,14},{8,16},{10,18},{12,20},{14,22},{16,24},... | collective-permute-start | bytes 786440 | tf_op jit(solution)/shard_map/ppermute | solution.py:370
  314.6 58.9 %collective-permute-start.22 = (bf16[2,512,128]{2,1,0:T(8,128)(2,1)S(1)}, bf16[2,512,128]{2,1,0:T(8,128)(2,1)S(1)}, u32[]{:S(2)}, u32[]{:S(2)}) collective-permute-start(bf16[2,512,128]{2,1,0:T(8,128)(2,1)S(1)} %copy-done.35), channel_id=1, source_target_pairs={{8,0},{10,2},{12,4},{14,6},{16,8},{18,10},{20,12},{22,14},{24,16},... | collective-permute-start | bytes 786440 | tf_op jit(solution)/shard_map/ppermute | solution.py:371
  317.1 69.5 %collective-permute-start.19 = (bf16[2,512,128]{2,1,0:T(8,128)(2,1)}, bf16[2,512,128]{2,1,0:T(8,128)(2,1)S(1)}, u32[]{:S(2)}, u32[]{:S(2)}) collective-permute-start(bf16[2,512,128]{2,1,0:T(8,128)(2,1)} %get-tuple-element.80), channel_id=1, source_target_pairs={{0,8},{2,10},{4,12},{6,14},{8,16},{10,18},{12,20},{14,22},{16,24},... | collective-permute-start | bytes 786440 | tf_op jit(solution)/shard_map/ppermute | solution.py:370
  358.3 28.3 %collective-permute-start.20 = (bf16[2,512,128]{2,1,0:T(8,128)(2,1)}, bf16[2,512,128]{2,1,0:T(8,128)(2,1)S(1)}, u32[]{:S(2)}, u32[]{:S(2)}) collective-permute-start(bf16[2,512,128]{2,1,0:T(8,128)(2,1)} %get-tuple-element.81), channel_id=1, source_target_pairs={{8,0},{10,2},{12,4},{14,6},{16,8},{18,10},{20,12},{22,14},{24,16},... | collective-permute-start | bytes 786440 | tf_op jit(solution)/shard_map/ppermute | solution.py:371
  (48 other events, 317.9 us)
where the time goes:
time: 419 us; the launch traced here: 417 us
  waiting for transfers between devices  202 us (48%)
  Pallas kernels  101 us (24%)
  starting transfers between devices  82.4 us (20%)
  local copies, waits for them, and re-layouts  20.8 us (5%)
  other arithmetic  6.7 us (2%)
    all_to_all x5, waiting for transfers between devices, exchange(): lax.all_to_all(far, 'tm', 0, 0, axis_index_groups=plan.lines(), tiled=True)  72.3 us
    ppermute x5, waiting for transfers between devices, exchange(): lax.ppermute(to_next, 'tm', plan.halo(1))  68.3 us
    ppermute x18, waiting for transfers between devices, share(): lax.ppermute(xs[j], 'tm', plan.swap(j))  61.8 us
    pallas_call x4, Pallas kernels, attend(): pl.pallas_call(functools.partial(attend_body, plan, items, at_out, len(ou...  57.5 us
    all_to_all x5, starting transfers between devices, exchange(): lax.all_to_all(far, 'tm', 0, 0, axis_index_groups=plan.lines(), tiled=True)  32.2 us
    pallas_call x4, Pallas kernels, select(): pl.pallas_call(functools.partial(select_body, scaled, len(after), plan.gr...  22.7 us
    ppermute x18, starting transfers between devices, share(): lax.ppermute(xs[j], 'tm', plan.swap(j))  21.2 us
    pallas_call x5, Pallas kernels, pack(): pl.pallas_call(functools.partial(pack_body, plan, len(after)), grid=(1,),...  16.3 us
  transfers between devices with their start and end apart: 33, of which 15 were waited for; matrix products, arithmetic and copies ran while one was open for 3% of the time, Pallas kernels for 19%

commit v1 on v0

--- a/solution.py
+++ b/solution.py
@@ -385,34 +385,39 @@
         rounds.append(list(range(2, heads - 1)))
     if heads > 2:
         rounds.append([heads - 1])
-    packed, recvs, where, after = [], [], [], []
-    out = None
+    packed, recvs, where, after, rest = [], [], [], [], []
+
+    def near():
+        return list(recvs[-1][1:]) if recvs else []
+
     for index, chosen in enumerate(rounds):
         items = [item for h in chosen for item in pair(h)]
         ending = index + 1 == len(rounds)
         x = share(select(plan, place, items + (queries if ending else []), after))
+        for old, n in rest:
+            recvs.append(exchange(old, n, near() + x))
         where += [(x, 2 * n) for n in range(len(chosen))]
-        if ending:
-            q, first_q = x, len(items)
-        else:
-            for n in range(len(chosen)):
-                recvs.append(exchange(x, n, []))
-                if n == 0:
-                    after = packed[-1]
+        if not ending:
+            recvs.append(exchange(x, 0, near()))
+            after = packed[-1]
+            rest = [(x, n) for n in range(1, len(chosen))]
     pos = far_positions(plan, plane, far_frames, far_pick)
 
     def run(chosen, at_out, of, out):
-        args = [(q, first_q + h, *where[h], recvs[h]) for h in chosen]
-        return attend(plan, place, pos, args, at_out, of, out)
+        args = [(x, len(items) + h, *where[h], recvs[h]) for h in chosen]
+        return list(attend(plan, place, pos, args, at_out, of, out))
 
     early = min(2, heads - 1)
+    first, out = [], []
     if early:
-        out = merge(plan, place, share(run(range(early), 0, early, [])), 0, [])
-    recvs.append(exchange(x, 0, [out] if early else []))
+        first = run(range(early), 0, early, [])
+    recvs.append(exchange(x, 0, near() + first))
+    if early:
+        out = [merge(plan, place, share(first), 0, [])]
     held = []
     for h in range(early, heads):
         held = run([h], h - early, heads - early, held)
-    return merge(plan, place, share(held), early, [out] if early else [])
+    return merge(plan, place, share(held), early, out)
 
 
 def solution(mesh):

time: 419 us -> 385 us (0.919)
  waiting for transfers between devices: 202 us -> 184 us
  starting transfers between devices: 82.4 us -> 74.7 us
  local copies, waits for them, and re-layouts: 20.8 us -> 13.5 us
    ppermute x5, waiting for transfers between devices: 68.3 us -> 142 us  [exchange(): lax.ppermute(to_next, 'tm', plan.halo(1))]
    all_to_all x5, waiting for transfers between devices: 72.3 us -> 0.01 us  [exchange(): lax.all_to_all(far, 'tm', 0, 0, axis_index_groups=plan.lines(), tiled=True)]
    ppermute x18, waiting for transfers between devices: 61.8 us -> 41.7 us  [share(): lax.ppermute(xs[j], 'tm', plan.swap(j))]
    all_to_all x5, starting transfers between devices: 32.2 us -> 23.2 us  [exchange(): lax.all_to_all(far, 'tm', 0, 0, axis_index_groups=plan.lines(), tiled=True)]
    unnamed x78 -> x94, local copies, waits for them, and re-layouts: 8.89 us -> 8.35 us
  transfers between devices with their start and end apart: 33 -> 33, of which waited for: 15 -> 11; matrix products, arithmetic and copies ran while one was open for 3% -> 1% of each run, Pallas kernels for 19% -> 24%
where the time goes in v1:
time: 385 us; the launch traced here: 381 us
  waiting for transfers between devices  184 us (48%)
  Pallas kernels  102 us (26%)
  starting transfers between devices  74.7 us (19%)
  local copies, waits for them, and re-layouts  13.5 us (4%)
  other arithmetic  4.34 us (1%)
    ppermute x5, waiting for transfers between devices, exchange(): lax.ppermute(to_next, 'tm', plan.halo(1))  142 us
    pallas_call x4, Pallas kernels, attend(): pl.pallas_call(functools.partial(attend_body, plan, items, at_out, len(ou...  57.7 us
    ppermute x18, waiting for transfers between devices, share(): lax.ppermute(xs[j], 'tm', plan.swap(j))  41.7 us
    pallas_call x4, Pallas kernels, select(): pl.pallas_call(functools.partial(select_body, scaled, len(after), plan.gr...  23.2 us
    all_to_all x5, starting transfers between devices, exchange(): lax.all_to_all(far, 'tm', 0, 0, axis_index_groups=plan.lines(), tiled=True)  23.2 us
    ppermute x18, starting transfers between devices, share(): lax.ppermute(xs[j], 'tm', plan.swap(j))  22.2 us
    pallas_call x5, Pallas kernels, pack(): pl.pallas_call(functools.partial(pack_body, plan, len(after)), grid=(1,),...  16.1 us
    ppermute x5, starting transfers between devices, exchange(): lax.ppermute(to_next, 'tm', plan.halo(1))  16 us
  transfers between devices with their start and end apart: 33, of which 11 were waited for; matrix products, arithmetic and copies ran while one was open for 1% of the time, Pallas kernels for 24%

profile of v1, /device:TPU:16, one launch (start us, length us, event | category | flops | bytes accessed | tf_op | source)
XLA Modules:
  0.0 381.3 jit_solution(12066912169652068128)
XLA Ops:
  7.7 4.5 %select.28 = (bf16[2,512,128]{2,1,0:T(8,128)(2,1)}, bf16[2,512,128]{2,1,0:T(8,128)(2,1)}, bf16[2,512,128]{2,1,0:T(8,128)(2,1)}, bf16[2,512,128]{2,1,0:T(8,128)(2,1)}) custom-call(s32[2]{0:T(128)} %pad_add_fusion.1.place_ref.refs_0_, bf16[512,2560]{1,0:T(8,128)(2,1)} %refs_0_.7, f32[512,1]{1,0:T(8,128)} %copy.63.refs_1_.refs_5_, ...), custom_call_target="tpu_custom_call" | custom-call | flops 1 | bytes 1 | tf_op jit(solution)/shard_map/select/pallas_call | solution.py:86
  16.3 5.3 %collective-permute-done.refs_1_.refs_7_ = bf16[2,512,128]{2,1,0:T(8,128)(2,1)S(1)} collective-permute-done((bf16[2,512,128]{2,1,0:T(8,128)(2,1)}, bf16[2,512,128]{2,1,0:T(8,128)(2,1)S(1)}, u32[]{:S(2)}, u32[]{:S(2)}) %collective-permute-start) | collective-permute-done | bytes 262176 | tf_op jit(solution)/shard_map/ppermute | solution.py:363
  21.6 6.1 %collective-permute-done.1.refs_2_.refs_8_ = bf16[2,512,128]{2,1,0:T(8,128)(2,1)S(1)} collective-permute-done((bf16[2,512,128]{2,1,0:T(8,128)(2,1)}, bf16[2,512,128]{2,1,0:T(8,128)(2,1)S(1)}, u32[]{:S(2)}, u32[]{:S(2)}) %collective-permute-start.1) | collective-permute-done | bytes 262176 | tf_op jit(solution)/shard_map/ppermute | solution.py:363
  31.7 5.2 %all-to-all-start = ((bf16[4,2,1024,128]{3,2,1,0:T(8,128)(2,1)}), bf16[4,2,1024,128]{3,2,1,0:T(8,128)(2,1)S(1)}, u32[]{:S(2)}, u32[]{:S(2)}) async-start(bf16[4,2,1024,128]{3,2,1,0:T(8,128)(2,1)} %get-tuple-element.56.refs_4_), calls=%async_computation | async-start | bytes 4194304 | tf_op jit(solution)/shard_map/all_to_all | solution.py:369
  36.9 4.5 %select.29 = (bf16[2,512,128]{2,1,0:T(8,128)(2,1)}, bf16[2,512,128]{2,1,0:T(8,128)(2,1)}, bf16[2,512,128]{2,1,0:T(8,128)(2,1)}, bf16[2,512,128]{2,1,0:T(8,128)(2,1)}) custom-call(s32[2]{0:T(128)} %pad_add_fusion.1.place_ref.refs_0_, bf16[512,2560]{1,0:T(8,128)(2,1)} %refs_0_.7, f32[512,1]{1,0:T(8,128)} %copy.63.refs_1_.refs_5_, ...), custom_call_target="tpu_custom_call" | custom-call | flops 1 | bytes 1 | tf_op jit(solution)/shard_map/select/pallas_call | solution.py:86
  44.9 3.4 collective-permute-start.6
  50.9 4.2 %collective-permute-done.4.refs_2_.refs_19_ = bf16[2,512,128]{2,1,0:T(8,128)(2,1)S(1)} collective-permute-done((bf16[2,512,128]{2,1,0:T(8,128)(2,1)}, bf16[2,512,128]{2,1,0:T(8,128)(2,1)S(1)}, u32[]{:S(2)}, u32[]{:S(2)}) %collective-permute-start.4) | collective-permute-done | bytes 262176 | tf_op jit(solution)/shard_map/ppermute | solution.py:363
  55.1 32.4 %collective-permute-done.6.refs_4_.refs_11_ = bf16[2,512,128]{2,1,0:T(8,128)(2,1)S(1)} collective-permute-done((bf16[2,512,128]{2,1,0:T(8,128)(2,1)S(1)}, bf16[2,512,128]{2,1,0:T(8,128)(2,1)S(1)}, u32[]{:S(2)}, u32[]{:S(2)}) %collective-permute-start.6) | collective-permute-done | bytes 262176 | tf_op jit(solution)/shard_map/ppermute | solution.py:370
  91.6 4.5 %all-to-all-start.1 = ((bf16[4,2,1024,128]{3,2,1,0:T(8,128)(2,1)}), bf16[4,2,1024,128]{3,2,1,0:T(8,128)(2,1)}, u32[]{:S(2)}, u32[]{:S(2)}) async-start(bf16[4,2,1024,128]{3,2,1,0:T(8,128)(2,1)} %get-tuple-element.63.refs_8_), calls=%async_computation.1 | async-start | bytes 4194304 | tf_op jit(solution)/shard_map/all_to_all | solution.py:369
  96.1 5.7 %select.30 = (bf16[4,512,128]{2,1,0:T(8,128)(2,1)}, bf16[4,512,128]{2,1,0:T(8,128)(2,1)}, bf16[4,512,128]{2,1,0:T(8,128)(2,1)}, bf16[4,512,128]{2,1,0:T(8,128)(2,1)}) custom-call(s32[2]{0:T(128)} %pad_add_fusion.1.place_ref.refs_0_, bf16[512,2560]{1,0:T(8,128)(2,1)} %refs_0_.7, f32[512,1]{1,0:T(8,128)} %copy.63.refs_1_.refs_5_, ...), custom_call_target="tpu_custom_call" | custom-call | flops 1 | bytes 1 | tf_op jit(solution)/shard_map/select/pallas_call | solution.py:86
  111.3 36.8 %collective-permute-done.11.refs_4_.refs_22_ = bf16[2,512,128]{2,1,0:T(8,128)(2,1)S(1)} collective-permute-done((bf16[2,512,128]{2,1,0:T(8,128)(2,1)S(1)}, bf16[2,512,128]{2,1,0:T(8,128)(2,1)S(1)}, u32[]{:S(2)}, u32[]{:S(2)}) %collective-permute-start.11) | collective-permute-done | bytes 262176 | tf_op jit(solution)/shard_map/ppermute | solution.py:370
  152.6 4.5 %all-to-all-start.4 = ((bf16[4,2,1024,128]{3,2,1,0:T(8,128)(2,1)}), bf16[4,2,1024,128]{3,2,1,0:T(8,128)(2,1)}, u32[]{:S(2)}, u32[]{:S(2)}) async-start(bf16[4,2,1024,128]{3,2,1,0:T(8,128)(2,1)} %get-tuple-element.70.refs_19_), calls=%async_computation.4 | async-start | bytes 4194304 | tf_op jit(solution)/shard_map/all_to_all | solution.py:369
  158.5 8.4 %select.31 = (bf16[7,512,128]{2,1,0:T(8,128)(2,1)}, bf16[7,512,128]{2,1,0:T(8,128)(2,1)}, bf16[7,512,128]{2,1,0:T(8,128)(2,1)}, bf16[7,512,128]{2,1,0:T(8,128)(2,1)}) custom-call(s32[2]{0:T(128)} %pad_add_fusion.1.place_ref.refs_0_, bf16[512,2560]{1,0:T(8,128)(2,1)} %refs_0_.7, f32[512,1]{1,0:T(8,128)} %copy.63.refs_1_.refs_5_, ...), custom_call_target="tpu_custom_call" | custom-call | flops 1 | bytes 1 | tf_op jit(solution)/shard_map/select/pallas_call | solution.py:86
  176.4 31.0 %collective-permute-done.16.refs_4_.refs_11_ = bf16[2,512,128]{2,1,0:T(8,128)(2,1)S(1)} collective-permute-done((bf16[2,512,128]{2,1,0:T(8,128)(2,1)S(1)}, bf16[2,512,128]{2,1,0:T(8,128)(2,1)S(1)}, u32[]{:S(2)}, u32[]{:S(2)}) %collective-permute-start.16) | collective-permute-done | bytes 262176 | tf_op jit(solution)/shard_map/ppermute | solution.py:370
  213.3 4.5 %all-to-all-start.3 = ((bf16[4,2,1024,128]{3,2,1,0:T(8,128)(2,1)}), bf16[4,2,1024,128]{3,2,1,0:T(8,128)(2,1)S(1)}, u32[]{:S(2)}, u32[]{:S(2)}) async-start(bf16[4,2,1024,128]{3,2,1,0:T(8,128)(2,1)} %get-tuple-element.86), calls=%async_computation.3 | async-start | bytes 4194304 | tf_op jit(solution)/shard_map/all_to_all | solution.py:369
  218.0 3.4 collective-permute-start.18
  226.1 20.7 %attend.4 = (bf16[2,512,128]{2,1,0:T(8,128)(2,1)}, bf16[2,512,128]{2,1,0:T(8,128)(2,1)}, bf16[2,512,128]{2,1,0:T(8,128)(2,1)}, bf16[2,512,128]{2,1,0:T(8,128)(2,1)}) custom-call(s32[2]{0:T(128)} %pad_add_fusion.1.place_ref.refs_0_, s32[192]{0:T(256)} %fusion.6.refs_1_, bf16[7,512,128]{2,1,0:T(8,128)(2,1)} %get-tuple-element.71.refs_6_.refs_2_.refs_13_.refs_0_, ...), custom_call_target="tpu_custom_call" | custom-call | flops 1 | bytes 1 | tf_op jit(solution)/shard_map/attend/pallas_call | solution.py:282
  246.8 22.6 %collective-permute-done.18.refs_4_.refs_11_ = bf16[2,512,128]{2,1,0:T(8,128)(2,1)S(1)} collective-permute-done((bf16[2,512,128]{2,1,0:T(8,128)(2,1)S(1)}, bf16[2,512,128]{2,1,0:T(8,128)(2,1)S(1)}, u32[]{:S(2)}, u32[]{:S(2)}) %collective-permute-start.18) | collective-permute-done | bytes 262176 | tf_op jit(solution)/shard_map/ppermute | solution.py:370
  273.5 4.6 %all-to-all-start.2 = ((bf16[4,2,1024,128]{3,2,1,0:T(8,128)(2,1)}), bf16[4,2,1024,128]{3,2,1,0:T(8,128)(2,1)}, u32[]{:S(2)}, u32[]{:S(2)}) async-start(bf16[4,2,1024,128]{3,2,1,0:T(8,128)(2,1)} %get-tuple-element.83), calls=%async_computation.2 | async-start | bytes 4194304 | tf_op jit(solution)/shard_map/all_to_all | solution.py:369
  285.5 12.3 %attend.5 = (bf16[3,512,128]{2,1,0:T(8,128)(2,1)}, bf16[3,512,128]{2,1,0:T(8,128)(2,1)}, bf16[3,512,128]{2,1,0:T(8,128)(2,1)}, bf16[3,512,128]{2,1,0:T(8,128)(2,1)}) custom-call(s32[2]{0:T(128)} %pad_add_fusion.1.place_ref.refs_0_, s32[192]{0:T(256)} %fusion.6.refs_1_, bf16[7,512,128]{2,1,0:T(8,128)(2,1)} %get-tuple-element.71.refs_6_.refs_2_.refs_13_.refs_0_, ...), custom_call_target="tpu_custom_call" | custom-call | flops 1 | bytes 1 | tf_op jit(solution)/shard_map/attend/pallas_call | solution.py:282
  297.7 12.3 %attend.6 = (bf16[3,512,128]{2,1,0:T(8,128)(2,1)}, bf16[3,512,128]{2,1,0:T(8,128)(2,1)}, bf16[3,512,128]{2,1,0:T(8,128)(2,1)}, bf16[3,512,128]{2,1,0:T(8,128)(2,1)}) custom-call(s32[2]{0:T(128)} %pad_add_fusion.1.place_ref.refs_0_, s32[192]{0:T(256)} %fusion.6.refs_1_, ...), custom_call_target="tpu_custom_call", output_to_operand_aliasing={{0}: (13, {}), {1}: (14, {}), {2}: (15, {}), {3}: (16, {})} | custom-call | flops 1 | bytes 1 | tf_op jit(solution)/shard_map/attend/pallas_call | solution.py:282
  310.0 19.2 %collective-permute-done.20.refs_11_ = bf16[2,512,128]{2,1,0:T(8,128)(2,1)S(1)} collective-permute-done((bf16[2,512,128]{2,1,0:T(8,128)(2,1)}, bf16[2,512,128]{2,1,0:T(8,128)(2,1)S(1)}, u32[]{:S(2)}, u32[]{:S(2)}) %collective-permute-start.20) | collective-permute-done | bytes 262176 | tf_op jit(solution)/shard_map/ppermute | solution.py:370
  330.0 12.5 %attend.7 = (bf16[3,512,128]{2,1,0:T(8,128)(2,1)}, bf16[3,512,128]{2,1,0:T(8,128)(2,1)}, bf16[3,512,128]{2,1,0:T(8,128)(2,1)}, bf16[3,512,128]{2,1,0:T(8,128)(2,1)}) custom-call(s32[2]{0:T(128)} %pad_add_fusion.1.place_ref.refs_0_, s32[192]{0:T(256)} %fusion.6.refs_1_, ...), custom_call_target="tpu_custom_call", output_to_operand_aliasing={{0}: (13, {}), {1}: (14, {}), {2}: (15, {}), {3}: (16, {})} | custom-call | flops 1 | bytes 1 | tf_op jit(solution)/shard_map/attend/pallas_call | solution.py:282
  349.0 24.8 %collective-permute-done.26.refs_2_ = bf16[2,512,128]{2,1,0:T(8,128)(2,1)S(1)} collective-permute-done((bf16[2,512,128]{2,1,0:T(8,128)(2,1)S(1)}, bf16[2,512,128]{2,1,0:T(8,128)(2,1)S(1)}, u32[]{:S(2)}, u32[]{:S(2)}) %collective-permute-start.26) | collective-permute-done | bytes 262176 | tf_op jit(solution)/shard_map/ppermute | solution.py:363
  (187 shorter events, 87.4 us)
Async XLA Ops:
  31.7 59.9 %all-to-all-start = ((bf16[4,2,1024,128]{3,2,1,0:T(8,128)(2,1)}), bf16[4,2,1024,128]{3,2,1,0:T(8,128)(2,1)S(1)}, u32[]{:S(2)}, u32[]{:S(2)}) async-start(bf16[4,2,1024,128]{3,2,1,0:T(8,128)(2,1)} %get-tuple-element.56.refs_4_), calls=%async_computation | async-start | bytes 4194304 | tf_op jit(solution)/shard_map/all_to_all | solution.py:369
  44.9 42.6 %collective-permute-start.6 = (bf16[2,512,128]{2,1,0:T(8,128)(2,1)S(1)}, bf16[2,512,128]{2,1,0:T(8,128)(2,1)S(1)}, u32[]{:S(2)}, u32[]{:S(2)}) collective-permute-start(bf16[2,512,128]{2,1,0:T(8,128)(2,1)S(1)} %copy-done.44), channel_id=1, source_target_pairs={{0,8},{2,10},{4,12},{6,14},{8,16},{10,18},{12,20},{14,22},{16,24},... | collective-permute-start | bytes 786440 | tf_op jit(solution)/shard_map/ppermute | solution.py:370
  48.3 39.2 %collective-permute-start.7 = (bf16[2,512,128]{2,1,0:T(8,128)(2,1)S(1)}, bf16[2,512,128]{2,1,0:T(8,128)(2,1)S(1)}, u32[]{:S(2)}, u32[]{:S(2)}) collective-permute-start(bf16[2,512,128]{2,1,0:T(8,128)(2,1)S(1)} %copy-done.42), channel_id=1, source_target_pairs={{8,0},{10,2},{12,4},{14,6},{16,8},{18,10},{20,12},{22,14},{24,16},... | collective-permute-start | bytes 786440 | tf_op jit(solution)/shard_map/ppermute | solution.py:371
  91.6 61.0 %all-to-all-start.1 = ((bf16[4,2,1024,128]{3,2,1,0:T(8,128)(2,1)}), bf16[4,2,1024,128]{3,2,1,0:T(8,128)(2,1)}, u32[]{:S(2)}, u32[]{:S(2)}) async-start(bf16[4,2,1024,128]{3,2,1,0:T(8,128)(2,1)} %get-tuple-element.63.refs_8_), calls=%async_computation.1 | async-start | bytes 4194304 | tf_op jit(solution)/shard_map/all_to_all | solution.py:369
  101.8 46.2 %collective-permute-start.10 = (bf16[4,512,128]{2,1,0:T(8,128)(2,1)}, bf16[4,512,128]{2,1,0:T(8,128)(2,1)S(1)}, u32[]{:S(2)}, u32[]{:S(2)}) collective-permute-start(bf16[4,512,128]{2,1,0:T(8,128)(2,1)} %get-tuple-element.67), channel_id=1, source_target_pairs={{0,6},{2,4},{4,2},{6,0},{8,14},{10,12},{12,10},{14,8},{16,22},{18,... | collective-permute-start | bytes 1572872 | tf_op jit(solution)/shard_map/ppermute | solution.py:363
  103.3 44.7 %collective-permute-start.8 = (bf16[4,512,128]{2,1,0:T(8,128)(2,1)}, bf16[4,512,128]{2,1,0:T(8,128)(2,1)S(1)}, u32[]{:S(2)}, u32[]{:S(2)}) collective-permute-start(bf16[4,512,128]{2,1,0:T(8,128)(2,1)} %get-tuple-element.65), channel_id=1, source_target_pairs={{0,2},{2,0},{4,6},{6,4},{8,10},{10,8},{12,14},{14,12},{16,18},{18,... | collective-permute-start | bytes 1572872 | tf_op jit(solution)/shard_map/ppermute | solution.py:363
  104.9 43.2 %collective-permute-start.9 = (bf16[4,512,128]{2,1,0:T(8,128)(2,1)}, bf16[4,512,128]{2,1,0:T(8,128)(2,1)S(1)}, u32[]{:S(2)}, u32[]{:S(2)}) collective-permute-start(bf16[4,512,128]{2,1,0:T(8,128)(2,1)} %get-tuple-element.66), channel_id=1, source_target_pairs={{0,4},{2,6},{4,0},{6,2},{8,12},{10,14},{12,8},{14,10},{16,20},{18,... | collective-permute-start | bytes 1572872 | tf_op jit(solution)/shard_map/ppermute | solution.py:363
  105.4 42.7 %collective-permute-start.11 = (bf16[2,512,128]{2,1,0:T(8,128)(2,1)S(1)}, bf16[2,512,128]{2,1,0:T(8,128)(2,1)S(1)}, u32[]{:S(2)}, u32[]{:S(2)}) collective-permute-start(bf16[2,512,128]{2,1,0:T(8,128)(2,1)S(1)} %copy-done.46), channel_id=1, source_target_pairs={{0,8},{2,10},{4,12},{6,14},{8,16},{10,18},{12,20},{14,22},{16,24},... | collective-permute-start | bytes 786440 | tf_op jit(solution)/shard_map/ppermute | solution.py:370
  108.5 39.6 %collective-permute-start.12 = (bf16[2,512,128]{2,1,0:T(8,128)(2,1)S(1)}, bf16[2,512,128]{2,1,0:T(8,128)(2,1)S(1)}, u32[]{:S(2)}, u32[]{:S(2)}) collective-permute-start(bf16[2,512,128]{2,1,0:T(8,128)(2,1)S(1)} %copy-done.45), channel_id=1, source_target_pairs={{8,0},{10,2},{12,4},{14,6},{16,8},{18,10},{20,12},{22,14},{24,16},... | collective-permute-start | bytes 786440 | tf_op jit(solution)/shard_map/ppermute | solution.py:371
  152.6 60.7 %all-to-all-start.4 = ((bf16[4,2,1024,128]{3,2,1,0:T(8,128)(2,1)}), bf16[4,2,1024,128]{3,2,1,0:T(8,128)(2,1)}, u32[]{:S(2)}, u32[]{:S(2)}) async-start(bf16[4,2,1024,128]{3,2,1,0:T(8,128)(2,1)} %get-tuple-element.70.refs_19_), calls=%async_computation.4 | async-start | bytes 4194304 | tf_op jit(solution)/shard_map/all_to_all | solution.py:369
  167.0 40.4 %collective-permute-start.13 = (bf16[7,512,128]{2,1,0:T(8,128)(2,1)}, bf16[7,512,128]{2,1,0:T(8,128)(2,1)S(1)}, u32[]{:S(2)}, u32[]{:S(2)}) collective-permute-start(bf16[7,512,128]{2,1,0:T(8,128)(2,1)} %get-tuple-element.72), channel_id=1, source_target_pairs={{0,2},{2,0},{4,6},{6,4},{8,10},{10,8},{12,14},{14,12},{16,18},{18,... | collective-permute-start | bytes 2752520 | tf_op jit(solution)/shard_map/ppermute | solution.py:363
  168.4 40.3 %collective-permute-start.14 = (bf16[7,512,128]{2,1,0:T(8,128)(2,1)}, bf16[7,512,128]{2,1,0:T(8,128)(2,1)S(1)}, u32[]{:S(2)}, u32[]{:S(2)}) collective-permute-start(bf16[7,512,128]{2,1,0:T(8,128)(2,1)} %get-tuple-element.73), channel_id=1, source_target_pairs={{0,4},{2,6},{4,0},{6,2},{8,12},{10,14},{12,8},{14,10},{16,20},{18,... | collective-permute-start | bytes 2752520 | tf_op jit(solution)/shard_map/ppermute | solution.py:363
  168.9 39.7 %collective-permute-start.15 = (bf16[7,512,128]{2,1,0:T(8,128)(2,1)}, bf16[7,512,128]{2,1,0:T(8,128)(2,1)S(1)}, u32[]{:S(2)}, u32[]{:S(2)}) collective-permute-start(bf16[7,512,128]{2,1,0:T(8,128)(2,1)} %get-tuple-element.74), channel_id=1, source_target_pairs={{0,6},{2,4},{4,2},{6,0},{8,14},{10,12},{12,10},{14,8},{16,22},{18,... | collective-permute-start | bytes 2752520 | tf_op jit(solution)/shard_map/ppermute | solution.py:363
  170.5 36.9 %collective-permute-start.16 = (bf16[2,512,128]{2,1,0:T(8,128)(2,1)S(1)}, bf16[2,512,128]{2,1,0:T(8,128)(2,1)S(1)}, u32[]{:S(2)}, u32[]{:S(2)}) collective-permute-start(bf16[2,512,128]{2,1,0:T(8,128)(2,1)S(1)} %copy-done.43), channel_id=1, source_target_pairs={{0,8},{2,10},{4,12},{6,14},{8,16},{10,18},{12,20},{14,22},{16,24},... | collective-permute-start | bytes 786440 | tf_op jit(solution)/shard_map/ppermute | solution.py:370
  173.6 33.8 %collective-permute-start.17 = (bf16[2,512,128]{2,1,0:T(8,128)(2,1)S(1)}, bf16[2,512,128]{2,1,0:T(8,128)(2,1)S(1)}, u32[]{:S(2)}, u32[]{:S(2)}) collective-permute-start(bf16[2,512,128]{2,1,0:T(8,128)(2,1)S(1)} %copy-done.41), channel_id=1, source_target_pairs={{8,0},{10,2},{12,4},{14,6},{16,8},{18,10},{20,12},{22,14},{24,16},... | collective-permute-start | bytes 786440 | tf_op jit(solution)/shard_map/ppermute | solution.py:371
  213.3 60.2 %all-to-all-start.3 = ((bf16[4,2,1024,128]{3,2,1,0:T(8,128)(2,1)}), bf16[4,2,1024,128]{3,2,1,0:T(8,128)(2,1)S(1)}, u32[]{:S(2)}, u32[]{:S(2)}) async-start(bf16[4,2,1024,128]{3,2,1,0:T(8,128)(2,1)} %get-tuple-element.86), calls=%async_computation.3 | async-start | bytes 4194304 | tf_op jit(solution)/shard_map/all_to_all | solution.py:369
  218.0 51.4 %collective-permute-start.18 = (bf16[2,512,128]{2,1,0:T(8,128)(2,1)S(1)}, bf16[2,512,128]{2,1,0:T(8,128)(2,1)S(1)}, u32[]{:S(2)}, u32[]{:S(2)}) collective-permute-start(bf16[2,512,128]{2,1,0:T(8,128)(2,1)S(1)} %copy-done.39), channel_id=1, source_target_pairs={{0,8},{2,10},{4,12},{6,14},{8,16},{10,18},{12,20},{14,22},{16,24},... | collective-permute-start | bytes 786440 | tf_op jit(solution)/shard_map/ppermute | solution.py:370
  221.4 48.0 %collective-permute-start.19 = (bf16[2,512,128]{2,1,0:T(8,128)(2,1)S(1)}, bf16[2,512,128]{2,1,0:T(8,128)(2,1)S(1)}, u32[]{:S(2)}, u32[]{:S(2)}) collective-permute-start(bf16[2,512,128]{2,1,0:T(8,128)(2,1)S(1)} %copy-done.38), channel_id=1, source_target_pairs={{8,0},{10,2},{12,4},{14,6},{16,8},{18,10},{20,12},{22,14},{24,16},... | collective-permute-start | bytes 786440 | tf_op jit(solution)/shard_map/ppermute | solution.py:371
  273.5 55.7 %all-to-all-start.2 = ((bf16[4,2,1024,128]{3,2,1,0:T(8,128)(2,1)}), bf16[4,2,1024,128]{3,2,1,0:T(8,128)(2,1)}, u32[]{:S(2)}, u32[]{:S(2)}) async-start(bf16[4,2,1024,128]{3,2,1,0:T(8,128)(2,1)} %get-tuple-element.83), calls=%async_computation.2 | async-start | bytes 4194304 | tf_op jit(solution)/shard_map/all_to_all | solution.py:369
  278.1 51.1 %collective-permute-start.20 = (bf16[2,512,128]{2,1,0:T(8,128)(2,1)}, bf16[2,512,128]{2,1,0:T(8,128)(2,1)S(1)}, u32[]{:S(2)}, u32[]{:S(2)}) collective-permute-start(bf16[2,512,128]{2,1,0:T(8,128)(2,1)} %get-tuple-element.84), channel_id=1, source_target_pairs={{0,8},{2,10},{4,12},{6,14},{8,16},{10,18},{12,20},{14,22},{16,24},... | collective-permute-start | bytes 786440 | tf_op jit(solution)/shard_map/ppermute | solution.py:370
  281.2 48.0 %collective-permute-start.21 = (bf16[2,512,128]{2,1,0:T(8,128)(2,1)S(1)}, bf16[2,512,128]{2,1,0:T(8,128)(2,1)S(1)}, u32[]{:S(2)}, u32[]{:S(2)}) collective-permute-start(bf16[2,512,128]{2,1,0:T(8,128)(2,1)S(1)} %copy-done.40), channel_id=1, source_target_pairs={{8,0},{10,2},{12,4},{14,6},{16,8},{18,10},{20,12},{22,14},{24,16},... | collective-permute-start | bytes 786440 | tf_op jit(solution)/shard_map/ppermute | solution.py:371
  284.0 63.6 %collective-permute-start.25 = (bf16[2,512,128]{2,1,0:T(8,128)(2,1)S(1)}, bf16[2,512,128]{2,1,0:T(8,128)(2,1)S(1)}, u32[]{:S(2)}, u32[]{:S(2)}) collective-permute-start(bf16[2,512,128]{2,1,0:T(8,128)(2,1)S(1)} %copy-done.28), channel_id=1, source_target_pairs={{0,2},{2,0},{4,6},{6,4},{8,10},{10,8},{12,14},{14,12},{16,18},{18,... | collective-permute-start | bytes 786440 | tf_op jit(solution)/shard_map/ppermute | solution.py:363
  342.5 35.0 %collective-permute-start.22 = (bf16[3,512,128]{2,1,0:T(8,128)(2,1)}, bf16[3,512,128]{2,1,0:T(8,128)(2,1)S(1)}, u32[]{:S(2)}, u32[]{:S(2)}) collective-permute-start(bf16[3,512,128]{2,1,0:T(8,128)(2,1)} %get-tuple-element.96), channel_id=1, source_target_pairs={{0,2},{2,0},{4,6},{6,4},{8,10},{10,8},{12,14},{14,12},{16,18},{18,... | collective-permute-start | bytes 1179656 | tf_op jit(solution)/shard_map/ppermute | solution.py:363
  344.0 33.5 %collective-permute-start.23 = (bf16[3,512,128]{2,1,0:T(8,128)(2,1)}, bf16[3,512,128]{2,1,0:T(8,128)(2,1)S(1)}, u32[]{:S(2)}, u32[]{:S(2)}) collective-permute-start(bf16[3,512,128]{2,1,0:T(8,128)(2,1)} %get-tuple-element.97), channel_id=1, source_target_pairs={{0,4},{2,6},{4,0},{6,2},{8,12},{10,14},{12,8},{14,10},{16,20},{18,... | collective-permute-start | bytes 1179656 | tf_op jit(solution)/shard_map/ppermute | solution.py:363
  (56 other events, 505.7 us)

commit v2 on v1

--- a/solution.py
+++ b/solution.py
@@ -162,12 +162,12 @@
     )(place, picks, *xs, *after)
 
 
-def attend_body(plan, heads, at_out, n_out, *refs):
+def attend_body(plan, heads, n_wait, *refs):
     place_ref, pos_ref = refs[:2]
     group, rows, nfar = plan.group, plan.rows, len(plan.slots)
     step = 2 * group + 3
     inputs = [refs[2 + h * step : 2 + (h + 1) * step] for h in range(len(heads))]
-    refs = refs[2 + len(heads) * step + n_out :]
+    refs = refs[2 + len(heads) * step + n_wait :]
     outs, (qbuf, kvbuf, obuf, fark, farv, sem, out_sem) = refs[:group], refs[group:]
     plane, lane = place_ref[0], place_ref[1]
     scale = math.log2(math.e) / math.sqrt(HEAD_DIM)
@@ -264,27 +264,25 @@
         lax.fori_loop(0, group, lambda f, c, h=h: (one_frame(f, h), c)[1], 0)
     made = []
     for j in range(group):
-        dst = outs[j].at[at_out : at_out + len(heads)]
-        made.append(pltpu.make_async_copy(obuf.at[lane ^ j], dst, out_sem.at[j]))
+        made.append(pltpu.make_async_copy(obuf.at[lane ^ j], outs[j], out_sem.at[j]))
     for copy in made:
         copy.start()
     for copy in made:
         copy.wait()
 
 
-def attend(plan, place, pos, heads, at_out, of, outs):
+def attend(plan, place, pos, heads, wait):
     nfar, count = len(plan.slots), len(heads)
     any_spec = pl.BlockSpec(memory_space=pl.ANY)
     smem = pl.BlockSpec(memory_space=pltpu.SMEM)
     args = [y for q, _, kv, _, recv in heads for y in (*q, *kv, *recv)]
     items = [(at_q, at_k) for _, at_q, _, at_k, _ in heads]
-    shape = jax.ShapeDtypeStruct((of, plan.rows, HEAD_DIM), jnp.bfloat16)
+    shape = jax.ShapeDtypeStruct((count, plan.rows, HEAD_DIM), jnp.bfloat16)
     return pl.pallas_call(
-        functools.partial(attend_body, plan, items, at_out, len(outs)),
-        in_specs=[smem, smem] + [any_spec] * (len(args) + len(outs)),
+        functools.partial(attend_body, plan, items, len(wait)),
+        in_specs=[smem, smem] + [any_spec] * (len(args) + len(wait)),
         out_specs=[any_spec] * plan.group,
         out_shape=[shape] * plan.group,
-        input_output_aliases={2 + len(args) + j: j for j in range(len(outs))},
         scratch_shapes=[
             pltpu.VMEM((2, plan.group, plan.rows, HEAD_DIM), jnp.bfloat16),
             pltpu.VMEM((2, 2, plan.total * BLOCK, HEAD_DIM), jnp.bfloat16),
@@ -296,7 +294,7 @@
         ],
         name="attend",
         **params(),
-    )(place, pos, *args, *outs)
+    )(place, pos, *args, *wait)
 
 
 def merge_body(plan, first, place_ref, *refs):
@@ -388,7 +386,7 @@
     packed, recvs, where, after, rest = [], [], [], [], []
 
     def near():
-        return list(recvs[-1][1:]) if recvs else []
+        return list(recvs[-2][1:]) if len(recvs) > 1 else []
 
     for index, chosen in enumerate(rounds):
         items = [item for h in chosen for item in pair(h)]
@@ -403,21 +401,21 @@
             rest = [(x, n) for n in range(1, len(chosen))]
     pos = far_positions(plan, plane, far_frames, far_pick)
 
-    def run(chosen, at_out, of, out):
+    def run(chosen, wait):
         args = [(x, len(items) + h, *where[h], recvs[h]) for h in chosen]
-        return list(attend(plan, place, pos, args, at_out, of, out))
+        return list(attend(plan, place, pos, args, wait))
 
     early = min(2, heads - 1)
     first, out = [], []
     if early:
-        first = run(range(early), 0, early, [])
+        first = run(range(early), [])
     recvs.append(exchange(x, 0, near() + first))
     if early:
-        out = [merge(plan, place, share(first), 0, [])]
-    held = []
-    for h in range(early, heads):
-        held = run([h], h - early, heads - early, held)
-    return merge(plan, place, share(held), early, out)
+        out = [merge(plan, place, share(first), 0, out)]
+    for h in range(early, heads - 1, 2):
+        chosen = range(h, min(h + 2, heads - 1))
+        out = [merge(plan, place, share(run(chosen, [])), h, out)]
+    return merge(plan, place, share(run([heads - 1], out)), heads - 1, out)
 
 
 def solution(mesh):

time: 385 us -> 386 us (level)
  starting transfers between devices: 74.7 us -> 80.9 us
    ppermute x5, waiting for transfers between devices: 142 us -> 97.4 us  [exchange(): lax.ppermute(to_next, 'tm', plan.halo(1))]
    ppermute x5, waiting for transfers between devices: 0.01 us -> 34.8 us  [exchange(): lax.ppermute(to_prev, 'tm', plan.halo(-1))]
    all_to_all x5, waiting for transfers between devices: 0.01 us -> 22 us  [exchange(): lax.all_to_all(far, 'tm', 0, 0, axis_index_groups=plan.lines(), tiled=True)]
    ppermute x18 -> x21, waiting for transfers between devices: 41.7 us -> 27.9 us  [share(): lax.ppermute(xs[j], 'tm', plan.swap(j))]
    pallas_call x4 -> x3, Pallas kernels: 57.7 us -> 53.7 us  [attend(): pl.pallas_call(functools.partial(attend_body, plan, items, len(wait)), in...]
    ppermute x18 -> x21, starting transfers between devices: 22.2 us -> 24.7 us  [share(): lax.ppermute(xs[j], 'tm', plan.swap(j))]
    unnamed x94 -> x102, local copies, waits for them, and re-layouts: 8.35 us -> 9.22 us
  transfers between devices with their start and end apart: 33 -> 36, of which waited for: 11 -> 14; matrix products, arithmetic and copies ran while one was open for 1% -> 1% of each run, Pallas kernels for 24% -> 20%
where the time goes in v2:
time: 386 us; the launch traced here: 384 us
  waiting for transfers between devices  182 us (47%)
  Pallas kernels  99.2 us (26%)
  starting transfers between devices  80.9 us (21%)
  local copies, waits for them, and re-layouts  14.4 us (4%)
  other arithmetic  4.36 us (1%)
    ppermute x5, waiting for transfers between devices, exchange(): lax.ppermute(to_next, 'tm', plan.halo(1))  97.4 us
    pallas_call x3, Pallas kernels, attend(): pl.pallas_call(functools.partial(attend_body, plan, items, len(wait)), in...  53.7 us
    ppermute x5, waiting for transfers between devices, exchange(): lax.ppermute(to_prev, 'tm', plan.halo(-1))  34.8 us
    ppermute x21, waiting for transfers between devices, share(): lax.ppermute(xs[j], 'tm', plan.swap(j))  27.9 us
    all_to_all x5, starting transfers between devices, exchange(): lax.all_to_all(far, 'tm', 0, 0, axis_index_groups=plan.lines(), tiled=True)  26.4 us
    ppermute x21, starting transfers between devices, share(): lax.ppermute(xs[j], 'tm', plan.swap(j))  24.7 us
    pallas_call x4, Pallas kernels, select(): pl.pallas_call(functools.partial(select_body, scaled, len(after), plan.gr...  22.9 us
    all_to_all x5, waiting for transfers between devices, exchange(): lax.all_to_all(far, 'tm', 0, 0, axis_index_groups=plan.lines(), tiled=True)  22 us
  transfers between devices with their start and end apart: 36, of which 14 were waited for; matrix products, arithmetic and copies ran while one was open for 1% of the time, Pallas kernels for 20%

profile of v2, /device:TPU:16, one launch (start us, length us, event | category | flops | bytes accessed | tf_op | source)
XLA Modules:
  0.0 384.2 jit_solution(13745717576304567713)
XLA Ops:
  7.8 4.5 %select.28 = (bf16[2,512,128]{2,1,0:T(8,128)(2,1)}, bf16[2,512,128]{2,1,0:T(8,128)(2,1)}, bf16[2,512,128]{2,1,0:T(8,128)(2,1)}, bf16[2,512,128]{2,1,0:T(8,128)(2,1)}) custom-call(s32[2]{0:T(128)} %pad_add_fusion.1.place_ref.refs_0_, bf16[512,2560]{1,0:T(8,128)(2,1)} %refs_0_.7, f32[512,1]{1,0:T(8,128)} %copy.56.refs_1_.refs_5_, ...), custom_call_target="tpu_custom_call" | custom-call | flops 1 | bytes 1 | tf_op jit(solution)/shard_map/select/pallas_call | solution.py:86
  16.4 5.2 %collective-permute-done.refs_1_.refs_7_ = bf16[2,512,128]{2,1,0:T(8,128)(2,1)S(1)} collective-permute-done((bf16[2,512,128]{2,1,0:T(8,128)(2,1)}, bf16[2,512,128]{2,1,0:T(8,128)(2,1)S(1)}, u32[]{:S(2)}, u32[]{:S(2)}) %collective-permute-start) | collective-permute-done | bytes 262176 | tf_op jit(solution)/shard_map/ppermute | solution.py:361
  21.6 6.1 %collective-permute-done.1.refs_2_.refs_8_ = bf16[2,512,128]{2,1,0:T(8,128)(2,1)S(1)} collective-permute-done((bf16[2,512,128]{2,1,0:T(8,128)(2,1)}, bf16[2,512,128]{2,1,0:T(8,128)(2,1)S(1)}, u32[]{:S(2)}, u32[]{:S(2)}) %collective-permute-start.1) | collective-permute-done | bytes 262176 | tf_op jit(solution)/shard_map/ppermute | solution.py:361
  31.7 5.2 %all-to-all-start = ((bf16[4,2,1024,128]{3,2,1,0:T(8,128)(2,1)}), bf16[4,2,1024,128]{3,2,1,0:T(8,128)(2,1)S(1)}, u32[]{:S(2)}, u32[]{:S(2)}) async-start(bf16[4,2,1024,128]{3,2,1,0:T(8,128)(2,1)} %get-tuple-element.52.refs_4_), calls=%async_computation | async-start | bytes 4194304 | tf_op jit(solution)/shard_map/all_to_all | solution.py:367
  36.9 4.4 %select.29 = (bf16[2,512,128]{2,1,0:T(8,128)(2,1)}, bf16[2,512,128]{2,1,0:T(8,128)(2,1)}, bf16[2,512,128]{2,1,0:T(8,128)(2,1)}, bf16[2,512,128]{2,1,0:T(8,128)(2,1)}) custom-call(s32[2]{0:T(128)} %pad_add_fusion.1.place_ref.refs_0_, bf16[512,2560]{1,0:T(8,128)(2,1)} %refs_0_.7, f32[512,1]{1,0:T(8,128)} %copy.56.refs_1_.refs_5_, ...), custom_call_target="tpu_custom_call" | custom-call | flops 1 | bytes 1 | tf_op jit(solution)/shard_map/select/pallas_call | solution.py:86
  44.9 6.0 %collective-permute-done.3.refs_1_.refs_18_ = bf16[2,512,128]{2,1,0:T(8,128)(2,1)S(1)} collective-permute-done((bf16[2,512,128]{2,1,0:T(8,128)(2,1)}, bf16[2,512,128]{2,1,0:T(8,128)(2,1)S(1)}, u32[]{:S(2)}, u32[]{:S(2)}) %collective-permute-start.3) | collective-permute-done | bytes 262176 | tf_op jit(solution)/shard_map/ppermute | solution.py:361
  50.8 4.2 %collective-permute-done.4.refs_2_.refs_19_ = bf16[2,512,128]{2,1,0:T(8,128)(2,1)S(1)} collective-permute-done((bf16[2,512,128]{2,1,0:T(8,128)(2,1)}, bf16[2,512,128]{2,1,0:T(8,128)(2,1)S(1)}, u32[]{:S(2)}, u32[]{:S(2)}) %collective-permute-start.4) | collective-permute-done | bytes 262176 | tf_op jit(solution)/shard_map/ppermute | solution.py:361
  59.1 21.9 %all-to-all-done.refs_10_ = bf16[4,2,1024,128]{3,2,1,0:T(8,128)(2,1)S(1)} async-done(((bf16[4,2,1024,128]{3,2,1,0:T(8,128)(2,1)}), bf16[4,2,1024,128]{3,2,1,0:T(8,128)(2,1)S(1)}, u32[]{:S(2)}, u32[]{:S(2)}) %all-to-all-start) | async-done | bytes 2097184 | tf_op jit(solution)/shard_map/all_to_all | solution.py:367
  81.1 7.7 %all-to-all-start.1 = ((bf16[4,2,1024,128]{3,2,1,0:T(8,128)(2,1)}), bf16[4,2,1024,128]{3,2,1,0:T(8,128)(2,1)}, u32[]{:S(2)}, u32[]{:S(2)}) async-start(bf16[4,2,1024,128]{3,2,1,0:T(8,128)(2,1)} %get-tuple-element.57.refs_8_), calls=%async_computation.1 | async-start | bytes 4194304 | tf_op jit(solution)/shard_map/all_to_all | solution.py:367
  88.8 5.7 %select.30 = (bf16[4,512,128]{2,1,0:T(8,128)(2,1)}, bf16[4,512,128]{2,1,0:T(8,128)(2,1)}, bf16[4,512,128]{2,1,0:T(8,128)(2,1)}, bf16[4,512,128]{2,1,0:T(8,128)(2,1)}) custom-call(s32[2]{0:T(128)} %pad_add_fusion.1.place_ref.refs_0_, bf16[512,2560]{1,0:T(8,128)(2,1)} %refs_0_.7, f32[512,1]{1,0:T(8,128)} %copy.56.refs_1_.refs_5_, ...), custom_call_target="tpu_custom_call" | custom-call | flops 1 | bytes 1 | tf_op jit(solution)/shard_map/select/pallas_call | solution.py:86
  100.5 3.4 collective-permute-start.9
  103.9 34.8 %collective-permute-done.10.refs_5_.refs_12_ = bf16[2,512,128]{2,1,0:T(8,128)(2,1)S(1)} collective-permute-done((bf16[2,512,128]{2,1,0:T(8,128)(2,1)S(1)}, bf16[2,512,128]{2,1,0:T(8,128)(2,1)S(1)}, u32[]{:S(2)}, u32[]{:S(2)}) %collective-permute-start.10) | collective-permute-done | bytes 262176 | tf_op jit(solution)/shard_map/ppermute | solution.py:369
  144.2 4.5 %all-to-all-start.3 = ((bf16[4,2,1024,128]{3,2,1,0:T(8,128)(2,1)}), bf16[4,2,1024,128]{3,2,1,0:T(8,128)(2,1)}, u32[]{:S(2)}, u32[]{:S(2)}) async-start(bf16[4,2,1024,128]{3,2,1,0:T(8,128)(2,1)} %get-tuple-element.64.refs_19_), calls=%async_computation.3 | async-start | bytes 4194304 | tf_op jit(solution)/shard_map/all_to_all | solution.py:367
  150.1 8.2 %select.31 = (bf16[7,512,128]{2,1,0:T(8,128)(2,1)}, bf16[7,512,128]{2,1,0:T(8,128)(2,1)}, bf16[7,512,128]{2,1,0:T(8,128)(2,1)}, bf16[7,512,128]{2,1,0:T(8,128)(2,1)}) custom-call(s32[2]{0:T(128)} %pad_add_fusion.1.place_ref.refs_0_, bf16[512,2560]{1,0:T(8,128)(2,1)} %refs_0_.7, f32[512,1]{1,0:T(8,128)} %copy.56.refs_1_.refs_5_, ...), custom_call_target="tpu_custom_call" | custom-call | flops 1 | bytes 1 | tf_op jit(solution)/shard_map/select/pallas_call | solution.py:86
  167.8 33.0 %collective-permute-done.16.refs_22_.refs_4_ = bf16[2,512,128]{2,1,0:T(8,128)(2,1)S(1)} collective-permute-done((bf16[2,512,128]{2,1,0:T(8,128)(2,1)S(1)}, bf16[2,512,128]{2,1,0:T(8,128)(2,1)S(1)}, u32[]{:S(2)}, u32[]{:S(2)}) %collective-permute-start.16) | collective-permute-done | bytes 262176 | tf_op jit(solution)/shard_map/ppermute | solution.py:368
  206.0 4.3 %all-to-all-start.4 = ((bf16[4,2,1024,128]{3,2,1,0:T(8,128)(2,1)}), bf16[4,2,1024,128]{3,2,1,0:T(8,128)(2,1)S(1)}, u32[]{:S(2)}, u32[]{:S(2)}) async-start(bf16[4,2,1024,128]{3,2,1,0:T(8,128)(2,1)} %get-tuple-element.80), calls=%async_computation.4 | async-start | bytes 4194304 | tf_op jit(solution)/shard_map/all_to_all | solution.py:367
  210.6 3.4 collective-permute-start.14
  218.6 20.7 %attend.3 = (bf16[2,512,128]{2,1,0:T(8,128)(2,1)}, bf16[2,512,128]{2,1,0:T(8,128)(2,1)}, bf16[2,512,128]{2,1,0:T(8,128)(2,1)}, bf16[2,512,128]{2,1,0:T(8,128)(2,1)}) custom-call(s32[2]{0:T(128)} %pad_add_fusion.1.place_ref.refs_0_, s32[192]{0:T(256)} %fusion.6.refs_1_, bf16[7,512,128]{2,1,0:T(8,128)(2,1)} %get-tuple-element.65.refs_2_.refs_13_.refs_0_.refs_6_, ...), custom_call_target="tpu_custom_call" | custom-call | flops 1 | bytes 1 | tf_op jit(solution)/shard_map/attend/pallas_call | solution.py:281
  239.4 21.0 %collective-permute-done.14.refs_4_.refs_11_ = bf16[2,512,128]{2,1,0:T(8,128)(2,1)S(1)} collective-permute-done((bf16[2,512,128]{2,1,0:T(8,128)(2,1)S(1)}, bf16[2,512,128]{2,1,0:T(8,128)(2,1)S(1)}, u32[]{:S(2)}, u32[]{:S(2)}) %collective-permute-start.14) | collective-permute-done | bytes 262176 | tf_op jit(solution)/shard_map/ppermute | solution.py:368
  264.5 4.7 %all-to-all-start.2 = ((bf16[4,2,1024,128]{3,2,1,0:T(8,128)(2,1)}), bf16[4,2,1024,128]{3,2,1,0:T(8,128)(2,1)}, u32[]{:S(2)}, u32[]{:S(2)}) async-start(bf16[4,2,1024,128]{3,2,1,0:T(8,128)(2,1)} %get-tuple-element.77), calls=%async_computation.2 | async-start | bytes 4194304 | tf_op jit(solution)/shard_map/all_to_all | solution.py:367
  278.9 42.4 %collective-permute-done.20.refs_22_ = bf16[2,512,128]{2,1,0:T(8,128)(2,1)S(1)} collective-permute-done((bf16[2,512,128]{2,1,0:T(8,128)(2,1)S(1)}, bf16[2,512,128]{2,1,0:T(8,128)(2,1)S(1)}, u32[]{:S(2)}, u32[]{:S(2)}) %collective-permute-start.20) | collective-permute-done | bytes 262176 | tf_op jit(solution)/shard_map/ppermute | solution.py:368
  322.7 20.7 %attend.4 = (bf16[2,512,128]{2,1,0:T(8,128)(2,1)}, bf16[2,512,128]{2,1,0:T(8,128)(2,1)}, bf16[2,512,128]{2,1,0:T(8,128)(2,1)}, bf16[2,512,128]{2,1,0:T(8,128)(2,1)}) custom-call(s32[2]{0:T(128)} %pad_add_fusion.1.place_ref.refs_0_, s32[192]{0:T(256)} %fusion.6.refs_1_, bf16[7,512,128]{2,1,0:T(8,128)(2,1)} %get-tuple-element.65.refs_2_.refs_13_.refs_0_.refs_6_, ...), custom_call_target="tpu_custom_call" | custom-call | flops 1 | bytes 1 | tf_op jit(solution)/shard_map/attend/pallas_call | solution.py:281
  348.9 4.1 %collective-permute-start.19 = (bf16[2,512,128]{2,1,0:T(8,128)(2,1)S(1)}, bf16[2,512,128]{2,1,0:T(8,128)(2,1)S(1)}, u32[]{:S(2)}, u32[]{:S(2)}) collective-permute-start(bf16[2,512,128]{2,1,0:T(8,128)(2,1)S(1)} %copy-done.45), channel_id=1, source_target_pairs={{8,0},{10,2},{12,4},{14,6},{16,8},{18,10},{20,12},{22,14},{24,16},... | collective-permute-start | bytes 786440 | tf_op jit(solution)/shard_map/ppermute | solution.py:369
  361.0 12.2 %attend.5 = (bf16[1,512,128]{2,1,0:T(8,128)(2,1)}, bf16[1,512,128]{2,1,0:T(8,128)(2,1)}, bf16[1,512,128]{2,1,0:T(8,128)(2,1)}, bf16[1,512,128]{2,1,0:T(8,128)(2,1)}) custom-call(s32[2]{0:T(128)} %pad_add_fusion.1.place_ref.refs_0_, s32[192]{0:T(256)} %fusion.6.refs_1_, bf16[7,512,128]{2,1,0:T(8,128)(2,1)} %get-tuple-element.65.refs_2_.refs_13_.refs_0_.refs_6_, ...), custom_call_target="tpu_custom_call" | custom-call | flops 1 | bytes 1 | tf_op jit(solution)/shard_map/attend/pallas_call | solution.py:281
  (201 shorter events, 94.9 us)
Async XLA Ops:
  13.8 13.9 %collective-permute-start.1 = (bf16[2,512,128]{2,1,0:T(8,128)(2,1)}, bf16[2,512,128]{2,1,0:T(8,128)(2,1)S(1)}, u32[]{:S(2)}, u32[]{:S(2)}) collective-permute-start(bf16[2,512,128]{2,1,0:T(8,128)(2,1)} %get-tuple-element.50), channel_id=1, source_target_pairs={{0,4},{2,6},{4,0},{6,2},{8,12},{10,14},{12,8},{14,10},{16,20},{18,... | collective-permute-start | bytes 786440 | tf_op jit(solution)/shard_map/ppermute | solution.py:361
  31.7 49.4 %all-to-all-start = ((bf16[4,2,1024,128]{3,2,1,0:T(8,128)(2,1)}), bf16[4,2,1024,128]{3,2,1,0:T(8,128)(2,1)S(1)}, u32[]{:S(2)}, u32[]{:S(2)}) async-start(bf16[4,2,1024,128]{3,2,1,0:T(8,128)(2,1)} %get-tuple-element.52.refs_4_), calls=%async_computation | async-start | bytes 4194304 | tf_op jit(solution)/shard_map/all_to_all | solution.py:367
  81.1 63.1 %all-to-all-start.1 = ((bf16[4,2,1024,128]{3,2,1,0:T(8,128)(2,1)}), bf16[4,2,1024,128]{3,2,1,0:T(8,128)(2,1)}, u32[]{:S(2)}, u32[]{:S(2)}) async-start(bf16[4,2,1024,128]{3,2,1,0:T(8,128)(2,1)} %get-tuple-element.57.refs_8_), calls=%async_computation.1 | async-start | bytes 4194304 | tf_op jit(solution)/shard_map/all_to_all | solution.py:367
  94.4 45.3 %collective-permute-start.6 = (bf16[4,512,128]{2,1,0:T(8,128)(2,1)}, bf16[4,512,128]{2,1,0:T(8,128)(2,1)S(1)}, u32[]{:S(2)}, u32[]{:S(2)}) collective-permute-start(bf16[4,512,128]{2,1,0:T(8,128)(2,1)} %get-tuple-element.59), channel_id=1, source_target_pairs={{0,2},{2,0},{4,6},{6,4},{8,10},{10,8},{12,14},{14,12},{16,18},{18,... | collective-permute-start | bytes 1572872 | tf_op jit(solution)/shard_map/ppermute | solution.py:361
  96.0 43.8 %collective-permute-start.7 = (bf16[4,512,128]{2,1,0:T(8,128)(2,1)}, bf16[4,512,128]{2,1,0:T(8,128)(2,1)S(1)}, u32[]{:S(2)}, u32[]{:S(2)}) collective-permute-start(bf16[4,512,128]{2,1,0:T(8,128)(2,1)} %get-tuple-element.60), channel_id=1, source_target_pairs={{0,4},{2,6},{4,0},{6,2},{8,12},{10,14},{12,8},{14,10},{16,20},{18,... | collective-permute-start | bytes 1572872 | tf_op jit(solution)/shard_map/ppermute | solution.py:361
  96.5 43.2 %collective-permute-start.8 = (bf16[4,512,128]{2,1,0:T(8,128)(2,1)}, bf16[4,512,128]{2,1,0:T(8,128)(2,1)S(1)}, u32[]{:S(2)}, u32[]{:S(2)}) collective-permute-start(bf16[4,512,128]{2,1,0:T(8,128)(2,1)} %get-tuple-element.61), channel_id=1, source_target_pairs={{0,6},{2,4},{4,2},{6,0},{8,14},{10,12},{12,10},{14,8},{16,22},{18,... | collective-permute-start | bytes 1572872 | tf_op jit(solution)/shard_map/ppermute | solution.py:361
  98.0 40.7 %collective-permute-start.10 = (bf16[2,512,128]{2,1,0:T(8,128)(2,1)S(1)}, bf16[2,512,128]{2,1,0:T(8,128)(2,1)S(1)}, u32[]{:S(2)}, u32[]{:S(2)}) collective-permute-start(bf16[2,512,128]{2,1,0:T(8,128)(2,1)S(1)} %copy-done.50), channel_id=1, source_target_pairs={{8,0},{10,2},{12,4},{14,6},{16,8},{18,10},{20,12},{22,14},{24,16},... | collective-permute-start | bytes 786440 | tf_op jit(solution)/shard_map/ppermute | solution.py:369
  100.5 39.2 %collective-permute-start.9 = (bf16[2,512,128]{2,1,0:T(8,128)(2,1)S(1)}, bf16[2,512,128]{2,1,0:T(8,128)(2,1)S(1)}, u32[]{:S(2)}, u32[]{:S(2)}) collective-permute-start(bf16[2,512,128]{2,1,0:T(8,128)(2,1)S(1)} %copy-done.49), channel_id=1, source_target_pairs={{0,8},{2,10},{4,12},{6,14},{8,16},{10,18},{12,20},{14,22},{16,24},... | collective-permute-start | bytes 786440 | tf_op jit(solution)/shard_map/ppermute | solution.py:368
  144.2 61.8 %all-to-all-start.3 = ((bf16[4,2,1024,128]{3,2,1,0:T(8,128)(2,1)}), bf16[4,2,1024,128]{3,2,1,0:T(8,128)(2,1)}, u32[]{:S(2)}, u32[]{:S(2)}) async-start(bf16[4,2,1024,128]{3,2,1,0:T(8,128)(2,1)} %get-tuple-element.64.refs_19_), calls=%async_computation.3 | async-start | bytes 4194304 | tf_op jit(solution)/shard_map/all_to_all | solution.py:367
  158.4 42.5 %collective-permute-start.11 = (bf16[7,512,128]{2,1,0:T(8,128)(2,1)}, bf16[7,512,128]{2,1,0:T(8,128)(2,1)S(1)}, u32[]{:S(2)}, u32[]{:S(2)}) collective-permute-start(bf16[7,512,128]{2,1,0:T(8,128)(2,1)} %get-tuple-element.66), channel_id=1, source_target_pairs={{0,2},{2,0},{4,6},{6,4},{8,10},{10,8},{12,14},{14,12},{16,18},{18,... | collective-permute-start | bytes 2752520 | tf_op jit(solution)/shard_map/ppermute | solution.py:361
  159.9 40.9 %collective-permute-start.12 = (bf16[7,512,128]{2,1,0:T(8,128)(2,1)}, bf16[7,512,128]{2,1,0:T(8,128)(2,1)S(1)}, u32[]{:S(2)}, u32[]{:S(2)}) collective-permute-start(bf16[7,512,128]{2,1,0:T(8,128)(2,1)} %get-tuple-element.67), channel_id=1, source_target_pairs={{0,4},{2,6},{4,0},{6,2},{8,12},{10,14},{12,8},{14,10},{16,20},{18,... | collective-permute-start | bytes 2752520 | tf_op jit(solution)/shard_map/ppermute | solution.py:361
  160.4 40.4 %collective-permute-start.13 = (bf16[7,512,128]{2,1,0:T(8,128)(2,1)}, bf16[7,512,128]{2,1,0:T(8,128)(2,1)S(1)}, u32[]{:S(2)}, u32[]{:S(2)}) collective-permute-start(bf16[7,512,128]{2,1,0:T(8,128)(2,1)} %get-tuple-element.68), channel_id=1, source_target_pairs={{0,6},{2,4},{4,2},{6,0},{8,14},{10,12},{12,10},{14,8},{16,22},{18,... | collective-permute-start | bytes 2752520 | tf_op jit(solution)/shard_map/ppermute | solution.py:361
  161.9 38.9 %collective-permute-start.16 = (bf16[2,512,128]{2,1,0:T(8,128)(2,1)S(1)}, bf16[2,512,128]{2,1,0:T(8,128)(2,1)S(1)}, u32[]{:S(2)}, u32[]{:S(2)}) collective-permute-start(bf16[2,512,128]{2,1,0:T(8,128)(2,1)S(1)} %copy-done.48), channel_id=1, source_target_pairs={{0,8},{2,10},{4,12},{6,14},{8,16},{10,18},{12,20},{14,22},{16,24},... | collective-permute-start | bytes 786440 | tf_op jit(solution)/shard_map/ppermute | solution.py:368
  165.1 35.7 %collective-permute-start.17 = (bf16[2,512,128]{2,1,0:T(8,128)(2,1)S(1)}, bf16[2,512,128]{2,1,0:T(8,128)(2,1)S(1)}, u32[]{:S(2)}, u32[]{:S(2)}) collective-permute-start(bf16[2,512,128]{2,1,0:T(8,128)(2,1)S(1)} %copy-done.47), channel_id=1, source_target_pairs={{8,0},{10,2},{12,4},{14,6},{16,8},{18,10},{20,12},{22,14},{24,16},... | collective-permute-start | bytes 786440 | tf_op jit(solution)/shard_map/ppermute | solution.py:369
  206.0 58.5 %all-to-all-start.4 = ((bf16[4,2,1024,128]{3,2,1,0:T(8,128)(2,1)}), bf16[4,2,1024,128]{3,2,1,0:T(8,128)(2,1)S(1)}, u32[]{:S(2)}, u32[]{:S(2)}) async-start(bf16[4,2,1024,128]{3,2,1,0:T(8,128)(2,1)} %get-tuple-element.80), calls=%async_computation.4 | async-start | bytes 4194304 | tf_op jit(solution)/shard_map/all_to_all | solution.py:367
  210.6 49.8 %collective-permute-start.14 = (bf16[2,512,128]{2,1,0:T(8,128)(2,1)S(1)}, bf16[2,512,128]{2,1,0:T(8,128)(2,1)S(1)}, u32[]{:S(2)}, u32[]{:S(2)}) collective-permute-start(bf16[2,512,128]{2,1,0:T(8,128)(2,1)S(1)} %copy-done.42), channel_id=1, source_target_pairs={{0,8},{2,10},{4,12},{6,14},{8,16},{10,18},{12,20},{14,22},{16,24},... | collective-permute-start | bytes 786440 | tf_op jit(solution)/shard_map/ppermute | solution.py:368
  214.0 46.4 %collective-permute-start.15 = (bf16[2,512,128]{2,1,0:T(8,128)(2,1)S(1)}, bf16[2,512,128]{2,1,0:T(8,128)(2,1)S(1)}, u32[]{:S(2)}, u32[]{:S(2)}) collective-permute-start(bf16[2,512,128]{2,1,0:T(8,128)(2,1)S(1)} %copy-done.41), channel_id=1, source_target_pairs={{8,0},{10,2},{12,4},{14,6},{16,8},{18,10},{20,12},{22,14},{24,16},... | collective-permute-start | bytes 786440 | tf_op jit(solution)/shard_map/ppermute | solution.py:369
  264.5 95.7 %all-to-all-start.2 = ((bf16[4,2,1024,128]{3,2,1,0:T(8,128)(2,1)}), bf16[4,2,1024,128]{3,2,1,0:T(8,128)(2,1)}, u32[]{:S(2)}, u32[]{:S(2)}) async-start(bf16[4,2,1024,128]{3,2,1,0:T(8,128)(2,1)} %get-tuple-element.77), calls=%async_computation.2 | async-start | bytes 4194304 | tf_op jit(solution)/shard_map/all_to_all | solution.py:367
  269.3 52.0 %collective-permute-start.20 = (bf16[2,512,128]{2,1,0:T(8,128)(2,1)S(1)}, bf16[2,512,128]{2,1,0:T(8,128)(2,1)S(1)}, u32[]{:S(2)}, u32[]{:S(2)}) collective-permute-start(bf16[2,512,128]{2,1,0:T(8,128)(2,1)S(1)} %copy-done.44), channel_id=1, source_target_pairs={{0,8},{2,10},{4,12},{6,14},{8,16},{10,18},{12,20},{14,22},{16,24},... | collective-permute-start | bytes 786440 | tf_op jit(solution)/shard_map/ppermute | solution.py:368
  272.4 48.8 %collective-permute-start.21 = (bf16[2,512,128]{2,1,0:T(8,128)(2,1)S(1)}, bf16[2,512,128]{2,1,0:T(8,128)(2,1)S(1)}, u32[]{:S(2)}, u32[]{:S(2)}) collective-permute-start(bf16[2,512,128]{2,1,0:T(8,128)(2,1)S(1)} %copy-done.43), channel_id=1, source_target_pairs={{8,0},{10,2},{12,4},{14,6},{16,8},{18,10},{20,12},{22,14},{24,16},... | collective-permute-start | bytes 786440 | tf_op jit(solution)/shard_map/ppermute | solution.py:369
  275.3 70.2 %collective-permute-start.25 = (bf16[2,512,128]{2,1,0:T(8,128)(2,1)S(1)}, bf16[2,512,128]{2,1,0:T(8,128)(2,1)S(1)}, u32[]{:S(2)}, u32[]{:S(2)}) collective-permute-start(bf16[2,512,128]{2,1,0:T(8,128)(2,1)S(1)} %copy-done.25), channel_id=1, source_target_pairs={{0,2},{2,0},{4,6},{6,4},{8,10},{10,8},{12,14},{14,12},{16,18},{18,... | collective-permute-start | bytes 786440 | tf_op jit(solution)/shard_map/ppermute | solution.py:361
  276.8 70.1 %collective-permute-start.26 = (bf16[2,512,128]{2,1,0:T(8,128)(2,1)S(1)}, bf16[2,512,128]{2,1,0:T(8,128)(2,1)S(1)}, u32[]{:S(2)}, u32[]{:S(2)}) collective-permute-start(bf16[2,512,128]{2,1,0:T(8,128)(2,1)S(1)} %copy-done.24), channel_id=1, source_target_pairs={{0,4},{2,6},{4,0},{6,2},{8,12},{10,14},{12,8},{14,10},{16,20},{18,... | collective-permute-start | bytes 786440 | tf_op jit(solution)/shard_map/ppermute | solution.py:361
  277.4 71.5 %collective-permute-start.27 = (bf16[2,512,128]{2,1,0:T(8,128)(2,1)S(1)}, bf16[2,512,128]{2,1,0:T(8,128)(2,1)S(1)}, u32[]{:S(2)}, u32[]{:S(2)}) collective-permute-start(bf16[2,512,128]{2,1,0:T(8,128)(2,1)S(1)} %copy-done.23), channel_id=1, source_target_pairs={{0,6},{2,4},{4,2},{6,0},{8,14},{10,12},{12,10},{14,8},{16,22},{18,... | collective-permute-start | bytes 786440 | tf_op jit(solution)/shard_map/ppermute | solution.py:361
  347.0 13.2 %collective-permute-start.18 = (bf16[2,512,128]{2,1,0:T(8,128)(2,1)S(1)}, bf16[2,512,128]{2,1,0:T(8,128)(2,1)S(1)}, u32[]{:S(2)}, u32[]{:S(2)}) collective-permute-start(bf16[2,512,128]{2,1,0:T(8,128)(2,1)S(1)} %copy-done.46), channel_id=1, source_target_pairs={{0,8},{2,10},{4,12},{6,14},{8,16},{10,18},{12,20},{14,22},{16,24},... | collective-permute-start | bytes 786440 | tf_op jit(solution)/shard_map/ppermute | solution.py:368
  (63 other events, 531.9 us)
